TPU v7x, 32 devices: a whole 2x2x4 slice. The times are simulated.
32 devices in a mesh: grp: 2 (over y), feat: 4 (over z), layer: 2 (over x), dec: 2 (over core).
Axes of the slice: x: 2, y: 2, z: 4, core: 2. Of those that a mesh axis runs over, the one named last changes fastest.
Arguments:
- clean_resid: bfloat16 [2, 224, 2304], P('layer', ('grp', 'feat', 'dec')), parts along dimension 1, may hold values from -6 to 6
- corrupt_resid: bfloat16 [2, 224, 2304], P('layer', ('grp', 'feat', 'dec')), parts along dimension 1, may hold values from -6 to 6
- enc_weight: bfloat16 [2, 2304, 2048], P('layer', None, ('feat', 'dec')), may hold values from -0.125 to 0.125
- enc_bias: float32 [2, 2048], P('layer', ('feat', 'dec')), may hold values from -0.8 to 0.4
- dec_weight: bfloat16 [2, 3, 2048, 2304], P('layer', None, ('feat', 'dec')), may hold values from -0.078125 to 0.078125
- dec_bias: float32 [2, 2304], P('layer'), may hold values from -3 to 3
- patch_index: int32 [2, 8, 16], P('layer', ('feat', 'dec')), may hold values from 0 to 255, as said below
Outputs:
- recon: bfloat16 [2, 224, 2304], P('layer', ('grp', 'feat', 'dec')), parts along dimension 1
There are 2 independent parts, one for each index of `grp`. A program takes and returns all parts, laid end to end along the dimension named above; an argument that names none is the same for every part. Nothing has to cross between parts.
Inputs may be any that keep to these rules, and one draw needn't show every extreme that they name: `patch_index`: for each layer and slab, 16 different feature numbers within the slab.
All inputs are finite; a program needn't handle non-finite values.
Results may differ from a plain program's by a relative error of at most 0.0043.
Values may be sent and summed in bfloat16 or wider, within the bound.
No kernel may reach another device: no remote copies, remote signals or barrier semaphores. Data moves between devices by JAX's collectives and lax.ppermute only.
A program may use at most 64 MiB of HBM per device.

v0:
```python
import jax
import jax.numpy as jnp
from jax import lax
from jax.sharding import PartitionSpec as P

REACH = 3


def shifted(value, axis, by):
    count = lax.axis_size(axis)
    pairs = [(i, i + by) for i in range(count) if 0 <= i + by < count]
    return lax.ppermute(value, axis, pairs)


def local(clean_resid, corrupt_resid, enc_weight, enc_bias, dec_weight, dec_bias, patch_index):
    weight = enc_weight[0]
    bias = enc_bias[0]
    picks = patch_index[0, 0]
    width = weight.shape[1]
    onehot = (picks[:, None] == jnp.arange(width, dtype=jnp.int32)[None, :]).astype(jnp.float32)
    patched = jnp.sum(onehot, axis=0) > 0.5
    pick_weight = jnp.take(weight, picks, axis=1)
    pick_bias = jnp.take(bias, picks)
    clean_all, corrupt_all = (
        lax.all_gather(clean_resid, ("feat", "dec"), axis=1, tiled=True),
        lax.all_gather(corrupt_resid, ("feat", "dec"), axis=1, tiled=True),
    )
    clean_pre = jnp.dot(clean_all[0], weight, preferred_element_type=jnp.float32) + bias
    corrupt_pre = (
        jnp.dot(corrupt_all[0], pick_weight, preferred_element_type=jnp.float32) + pick_bias
    )
    spread = jnp.dot(jax.nn.relu(corrupt_pre), onehot, precision=lax.Precision.HIGHEST)
    features = jnp.where(patched[None, :], spread, jax.nn.relu(clean_pre)).astype(jnp.bfloat16)
    depth = min(REACH - 1, lax.axis_size("layer") - 1)
    known = [features]
    for offset in range(1, depth + 1):
        known.append(shifted(features, "layer", offset))
    for filler in range(REACH - len(known)):
        known.append(jnp.zeros_like(features))
    stacked = jnp.concatenate(known, axis=1)
    decoder = dec_weight[0].reshape(REACH * width, dec_weight.shape[3])
    summed = lax.psum_scatter(
        jnp.dot(stacked, decoder, preferred_element_type=jnp.float32),
        ("feat", "dec"),
        scatter_dimension=0,
        tiled=True,
    )
    return (summed + dec_bias[0]).astype(jnp.bfloat16)[None]


def solution(mesh):
    placed = (
        P("layer", ("grp", "feat", "dec"), None),
        P("layer", ("grp", "feat", "dec"), None),
        P("layer", None, ("feat", "dec")),
        P("layer", ("feat", "dec")),
        P("layer", None, ("feat", "dec"), None),
        P("layer", None),
        P("layer", ("feat", "dec"), None),
    )
    return jax.shard_map(
        local,
        mesh=mesh,
        in_specs=placed,
        out_specs=P("layer", ("grp", "feat", "dec"), None),
        check_vma=False,
    )
```

profile of v0, /device:TPU:0, one launch (start us, length us, event | category | flops | bytes accessed | tf_op | source)
XLA Modules:
  0.0 86.8 jit_solution(18248438868690926743)
XLA Ops:
  0.0 0.0 copy-start
  0.0 0.8 fusion.33
  0.8 1.5 %gather_fusion.1 = f32[16]{0:T(128)S(1)} fusion(f32[256]{0:T(256)} %bitcast.35, s32[1024]{0:T(1024)S(1)} %pad_clamp_fusion), kind=kCustom, calls=%fused_computation.1 | custom fusion | bytes 192 | tf_op jit(solution)/shard_map/jit(_take)/gather | solution.py:23
  2.3 0.7 broadcast_select_fusion
  3.0 2.4 %copy.16 = bf16[1,2304,256]{1,2,0:T(8,128)(2,1)} copy(bf16[1,2304,256]{2,1,0:T(8,128)(2,1)} %param.9) | data formatting | bytes 2359296 | tf_op args[2]
  5.4 2.7 %gather_fusion = bf16[16,2304]{1,0:T(8,128)(2,1)} fusion(bf16[2304,256]{0,1:T(8,128)(2,1)} %bitcast.37, s32[1024]{0:T(1024)S(1)} %pad_clamp_fusion), kind=kCustom, calls=%fused_computation | custom fusion | bytes 147520 | tf_op jit(solution)/shard_map/jit(_take)/gather | solution.py:22
  8.1 0.0 copy-start.5
  8.1 0.0 copy-start.3
  8.1 0.0 copy-start.4
  8.1 1.0 %copy.17 = bf16[1,14,2304]{2,0,1:T(2,128)(2,1)S(1)} copy(bf16[1,14,2304]{2,1,0:T(8,128)(2,1)} %param.8) | data formatting | bytes 129024 | tf_op args[1]
  9.1 18.2 %all_gather.6 = bf16[1,112,2304]{2,0,1:T(2,128)(2,1)S(1)} all-gather(bf16[1,14,2304]{2,0,1:T(2,128)(2,1)S(1)} %copy.17), channel_id=1, replica_groups=mesh['grp'=2,'feat'=4,'layer'=2,'dec'=2] {'feat','dec'}, dimensions={1}, use_global_device_ids=true | all-gather | bytes 580608 | tf_op jit(solution)/shard_map/all_gather | solution.py:26
  27.4 0.0 copy-start.1
  27.4 0.0 copy-start.2
  27.4 0.0 copy-done.5
  27.4 0.1 convert_reduce_fusion
  27.5 0.0 copy-done.3
  27.5 0.3 fusion.15
  27.7 0.3 fusion.31
  28.0 0.0 copy-done.4
  28.1 0.1 copy.18
  28.2 17.4 %all_gather.7 = bf16[1,112,2304]{2,0,1:T(2,128)(2,1)S(1)} all-gather(bf16[1,14,2304]{2,0,1:T(2,128)(2,1)S(1)} %copy.18), channel_id=1, replica_groups=mesh['grp'=2,'feat'=4,'layer'=2,'dec'=2] {'feat','dec'}, dimensions={1}, use_global_device_ids=true | all-gather | bytes 580608 | tf_op jit(solution)/shard_map/all_gather | solution.py:25
  45.5 0.0 copy-done.1
  45.5 0.0 copy-done.2
  45.5 0.3 fusion.12
  45.9 3.4 %collective-permute-start = (bf16[112,256]{1,0:T(8,128)(2,1)S(1)}, bf16[112,256]{1,0:T(8,128)(2,1)S(1)}, u32[]{:S(2)}, u32[]{:S(2)}) collective-permute-start(bf16[112,256]{1,0:T(8,128)(2,1)S(1)} %fusion.12), channel_id=1, source_target_pairs={{0,2},{1,3},{4,6},{5,7},{8,10},{9,11},{12,14},{13,15},{16,18},{17,... | collective-permute-start | bytes 172040 | tf_op jit(solution)/shard_map/ppermute | solution.py:12
  49.3 1.8 %collective-permute-done = bf16[112,256]{1,0:T(8,128)(2,1)S(1)} collective-permute-done((bf16[112,256]{1,0:T(8,128)(2,1)S(1)}, bf16[112,256]{1,0:T(8,128)(2,1)S(1)}, u32[]{:S(2)}, u32[]{:S(2)}) %collective-permute-start) | collective-permute-done | bytes 57376 | tf_op jit(solution)/shard_map/ppermute | solution.py:12
  51.1 0.0 copy-done
  51.1 1.7 %fusion.20 = f32[112,2304]{1,0:T(8,128)} fusion(bf16[768,2304]{1,0:T(8,128)(2,1)S(1)} %bitcast.34, bf16[112,256]{1,0:T(8,128)(2,1)S(1)} %collective-permute-done, bf16[112,256]{1,0:T(8,128)(2,1)S(1)} %fusion.12, bf16[768]{0:T(1024)(128)(2,1)S(1)} %pad.2.clone), kind=kOutput, calls=%fused_computation.14 | convolution fusion | flops 396877824 | bytes 4687360 | tf_op jit(solution)/shard_map/dot_general | solution.py:43
  52.8 0.0 copy-start.6
  52.8 23.7 %fusion = f32[16,2304]{1,0:T(8,128)} fusion(f32[112,2304]{1,0:T(8,128)} %fusion.20), kind=kCustom, calls=%all-reduce-scatter | all-reduce-scatter fusion | flops 294913 | bytes 1180160
  76.5 1.6 %slice.4 = f32[14,2304]{1,0:T(8,128)} slice(f32[16,2304]{1,0:T(8,128)} %fusion), slice={[2:16], [0:2304]} | slice | bytes 258048
  78.0 1.9 %collective-permute-start.1 = (f32[14,2304]{1,0:T(8,128)}, f32[14,2304]{1,0:T(8,128)}, u32[]{:S(2)}, u32[]{:S(2)}) collective-permute-start(f32[14,2304]{1,0:T(8,128)} %slice.4), channel_id=1, source_target_pairs={{0,1},{1,4},{4,5},{5,8},{8,9},{9,12},{12,13},{2,3},{3,6},{6,7},{7,... | collective-permute-start | bytes 387080
  80.0 0.0 copy-done.6
  80.0 0.6 dynamic-slice.4
  81.2 0.7 reduce
  81.9 0.0 collective-permute-done.1
  82.0 3.2 %concatenate.4 = f32[30,2304]{1,0:T(8,128)} concatenate(f32[14,2304]{1,0:T(8,128)} %collective-permute-done.1, f32[16,2304]{1,0:T(8,128)} %fusion), dimensions={0} | concatenate | bytes 552960
  85.2 1.6 %fusion.27 = bf16[1,14,2304]{2,1,0:T(8,128)(2,1)} fusion(f32[30,2304]{1,0:T(8,128)} %concatenate.4, u32[]{:S(6)} %subtract, f32[2304]{0:T(1024)S(1)} %reduce), kind=kLoop, calls=%fused_computation.22 | loop fusion | flops 64512 | bytes 202756 | tf_op jit(solution)/shard_map/broadcast_in_dim | solution.py:48
  (4 shorter events, 0.0 us)
Async XLA Ops:
  0.0 51.1 %copy-start = (bf16[1,3,256,2304]{3,2,1,0:T(8,128)(2,1)S(1)}, bf16[1,3,256,2304]{3,2,1,0:T(8,128)(2,1)}, u32[]{:S(2)}) copy-start(bf16[1,3,256,2304]{3,2,1,0:T(8,128)(2,1)} %param.11) | copy-start | bytes 10616836
  8.1 19.3 %copy-start.5 = (s32[1,1,16]{2,1,0:T(1,128)S(1)}, s32[1,1,16]{2,1,0:T(1,128)}, u32[]{:S(2)}) copy-start(s32[1,1,16]{2,1,0:T(1,128)} %param.13) | copy-start | bytes 196
  8.1 19.4 %copy-start.3 = (bf16[16,2304]{1,0:T(8,128)(2,1)S(1)}, bf16[16,2304]{1,0:T(8,128)(2,1)}, u32[]{:S(2)}) copy-start(bf16[16,2304]{1,0:T(8,128)(2,1)} %gather_fusion) | copy-start | bytes 221188
  8.1 20.0 %copy-start.4 = (bf16[1,14,2304]{2,1,0:T(8,128)(2,1)S(1)}, bf16[1,14,2304]{2,1,0:T(8,128)(2,1)}, u32[]{:S(2)}) copy-start(bf16[1,14,2304]{2,1,0:T(8,128)(2,1)} %param.7) | copy-start | bytes 193540
  27.4 18.2 %copy-start.1 = (f32[1,256]{1,0:T(1,128)S(1)}, f32[1,256]{1,0:T(1,128)}, u32[]{:S(2)}) copy-start(f32[1,256]{1,0:T(1,128)} %param.10) | copy-start | bytes 3076
  27.4 18.2 %copy-start.2 = (bf16[1,2304,256]{2,1,0:T(8,128)(2,1)S(1)}, bf16[1,2304,256]{2,1,0:T(8,128)(2,1)}, u32[]{:S(2)}) copy-start(bf16[1,2304,256]{2,1,0:T(8,128)(2,1)} %param.9) | copy-start | bytes 3538948
  45.9 5.2 %collective-permute-start = (bf16[112,256]{1,0:T(8,128)(2,1)S(1)}, bf16[112,256]{1,0:T(8,128)(2,1)S(1)}, u32[]{:S(2)}, u32[]{:S(2)}) collective-permute-start(bf16[112,256]{1,0:T(8,128)(2,1)S(1)} %fusion.12), channel_id=1, source_target_pairs={{0,2},{1,3},{4,6},{5,7},{8,10},{9,11},{12,14},{13,15},{16,18},{17,... | collective-permute-start | bytes 172040 | tf_op jit(solution)/shard_map/ppermute | solution.py:12
  52.8 27.2 %copy-start.6 = (u32[32]{0:T(128)S(1)}, u32[32]{0:T(128)}, u32[]{:S(2)}) copy-start(u32[32]{0:T(128)} %constant.48) | copy-start | bytes 388
  78.0 3.9 %collective-permute-start.1 = (f32[14,2304]{1,0:T(8,128)}, f32[14,2304]{1,0:T(8,128)}, u32[]{:S(2)}, u32[]{:S(2)}) collective-permute-start(f32[14,2304]{1,0:T(8,128)} %slice.4), channel_id=1, source_target_pairs={{0,1},{1,4},{4,5},{5,8},{8,9},{9,12},{12,13},{2,3},{3,6},{6,7},{7,... | collective-permute-start | bytes 387080
where the time goes:
time: 87.3 us; the launch traced here: 86.8 us
  blocking collectives  59.3 us (68%)
  local copies, waits for them, and re-layouts  13.2 us (15%)
  starting transfers between devices  5.33 us (6%)
  other arithmetic  3.89 us (4%)
  matrix products  2.56 us (3%)
  waiting for transfers between devices  1.79 us (2%)
    unnamed x1, blocking collectives  23.7 us
    all_gather x1, blocking collectives, local(): lax.all_gather(corrupt_resid, ('feat', 'dec'), axis=1, tiled=True)  18.2 us
    all_gather x1, blocking collectives, local(): lax.all_gather(clean_resid, ('feat', 'dec'), axis=1, tiled=True)  17.4 us
    unnamed x20, local copies, waits for them, and re-layouts  8.91 us
    ppermute x1, starting transfers between devices, shifted(): return lax.ppermute(value, axis, pairs)  3.39 us
    gather x1, local copies, waits for them, and re-layouts, local(): pick_weight = jnp.take(weight, picks, axis=1)  2.72 us
    unnamed x1, starting transfers between devices  1.94 us
    ppermute x1, waiting for transfers between devices, shifted(): return lax.ppermute(value, axis, pairs)  1.78 us
  transfers between devices with their start and end apart: 2, of which 1 were waited for; matrix products, arithmetic and copies ran while one was open for 2% of the time, Pallas kernels for 0%

commit v1 on v0

v1 whole, which is shorter than its diff:
```python
import jax
import jax.numpy as jnp
from jax import lax
from jax.sharding import PartitionSpec as P

REACH = 3


def moved(value, axis, pairs):
    return lax.ppermute(value, axis, pairs)


def shifted(value, axis, by):
    count = lax.axis_size(axis)
    return moved(value, axis, [(i, i + by) for i in range(count) if 0 <= i + by < count])


def rotated(value, axis, by):
    count = lax.axis_size(axis)
    return moved(value, axis, [(i, (i + by) % count) for i in range(count)])


def local(clean_resid, corrupt_resid, enc_weight, enc_bias, dec_weight, dec_bias, patch_index):
    chips = lax.axis_size("feat")
    cores = lax.axis_size("dec")
    depth = min(REACH - 1, lax.axis_size("layer") - 1)
    width = enc_weight.shape[2]
    rows, model = clean_resid.shape[1:]
    both = jnp.stack([clean_resid[0], corrupt_resid[0]])
    got = [both] + [rotated(both, "feat", k) for k in range(1, chips)]
    picks = patch_index[0, 0]
    mark = jnp.any(picks[:, None] == jnp.arange(width, dtype=jnp.int32)[None, :], axis=0)
    small = jnp.concatenate([enc_bias, mark.astype(jnp.float32)[None]], axis=0)
    smalls = [small] + [rotated(small, "dec", j) for j in range(1, cores)]
    encs = [enc_weight[0]] + [rotated(enc_weight[0], "dec", j) for j in range(1, cores)]
    decw = dec_weight[0, : depth + 1]
    decs = [decw] + [rotated(decw, "dec", j) for j in range(1, cores)]
    tokens = jnp.concatenate(got, axis=1)
    clean_all, corrupt_all = tokens[0], tokens[1]
    feats = []
    for w, s in zip(encs, smalls):
        c = jnp.dot(clean_all, w, preferred_element_type=jnp.float32)
        d = jnp.dot(corrupt_all, w, preferred_element_type=jnp.float32)
        pre = jnp.where(s[1][None] > 0.5, d, c) + s[0][None]
        feats.append(jax.nn.relu(pre).astype(jnp.bfloat16))
    stacked = jnp.concatenate(feats, axis=1)
    known = [stacked] + [shifted(stacked, "layer", o) for o in range(1, depth + 1)]
    total = 0.0
    for k in range(depth + 1):
        for j in range(cores):
            total = total + jnp.dot(
                known[k][:, j * width : (j + 1) * width],
                decs[j][k],
                preferred_element_type=jnp.float32,
            )
    summed = total[:rows]
    for k in range(1, chips):
        part = total[k * rows : (k + 1) * rows].astype(jnp.bfloat16)
        summed = summed + rotated(part, "feat", -k).astype(jnp.float32)
    return (summed + dec_bias).astype(jnp.bfloat16)[None]


def solution(mesh):
    placed = (
        P("layer", ("grp", "feat", "dec"), None),
        P("layer", ("grp", "feat", "dec"), None),
        P("layer", None, ("feat", "dec")),
        P("layer", ("feat", "dec")),
        P("layer", None, ("feat", "dec"), None),
        P("layer", None),
        P("layer", ("feat", "dec"), None),
    )
    return jax.shard_map(
        local,
        mesh=mesh,
        in_specs=placed,
        out_specs=P("layer", ("grp", "feat", "dec"), None),
        check_vma=False,
    )
```

time: 87.3 us -> 38.3 us (0.44)
  blocking collectives: 59.3 us -> 0 us
  starting transfers between devices: 5.33 us -> 17.9 us
  waiting for transfers between devices: 1.79 us -> 14.3 us
  local copies, waits for them, and re-layouts: 13.2 us -> 2.03 us
  other arithmetic: 3.89 us -> 1.01 us
    all_gather x2 -> x0, blocking collectives: 35.6 us -> none  [the longest x1 18.2 us: local(): lax.all_gather(corrupt_resid, ('feat', 'dec'), axis=1, tiled=True)]
    unnamed x1 -> x0, blocking collectives: 23.7 us -> none
    ppermute x1 -> x10, starting transfers between devices: 3.39 us -> 17.9 us  [moved(): return lax.ppermute(value, axis, pairs)]
    ppermute x1 -> x10, waiting for transfers between devices: 1.78 us -> 14.3 us  [moved(): return lax.ppermute(value, axis, pairs)]
    unnamed x20 -> x17, local copies, waits for them, and re-layouts: 8.91 us -> 0.04 us
    gather x2 -> x0, local copies, waits for them, and re-layouts: 4.24 us -> none  [the longest x1 2.72 us: local(): pick_weight = jnp.take(weight, picks, axis=1)]
    unnamed x1 -> x0, starting transfers between devices: 1.94 us -> none
    squeeze x0 -> x1, local copies, waits for them, and re-layouts: none -> 1.92 us  [local(): decw = dec_weight[0, :depth + 1]]
  transfers between devices with their start and end apart: 2 -> 10, of which waited for: 1 -> 6; matrix products, arithmetic and copies ran while one was open for 2% -> 5% of each run, Pallas kernels for 0% -> 0%
where the time goes in v1:
time: 38.3 us; the launch traced here: 38.2 us
  starting transfers between devices  17.9 us (47%)
  waiting for transfers between devices  14.3 us (37%)
  matrix products  2.7 us (7%)
  local copies, waits for them, and re-layouts  2.03 us (5%)
  other arithmetic  1.01 us (3%)
    ppermute x10, starting transfers between devices, moved(): return lax.ppermute(value, axis, pairs)  17.9 us
    ppermute x10, waiting for transfers between devices, moved(): return lax.ppermute(value, axis, pairs)  14.3 us
    squeeze x1, local copies, waits for them, and re-layouts, local(): decw = dec_weight[0, :depth + 1]  1.92 us
    dot_general x4, matrix products, local(): jnp.dot(known[k][:, j * width:(j + 1) * width], decs[j][k], preferred_ele...  1.34 us
  transfers between devices with their start and end apart: 10, of which 6 were waited for; matrix products, arithmetic and copies ran while one was open for 5% of the time, Pallas kernels for 0%

profile of v1, /device:TPU:0, one launch (start us, length us, event | category | flops | bytes accessed | tf_op | source)
XLA Modules:
  0.0 38.2 jit_solution(6413566524642257895)
XLA Ops:
  0.0 0.0 copy-start.1
  0.0 0.0 copy-start.7
  0.0 0.0 copy-start.6
  0.0 1.9 %slice_bitcast_fusion = bf16[2,256,2304]{2,1,0:T(8,128)(2,1)S(1)} fusion(bf16[1,3,256,2304]{3,2,1,0:T(8,128)(2,1)} %param.11), kind=kLoop, calls=%fused_computation.3 | loop fusion | bytes 4718592 | tf_op jit(solution)/shard_map/squeeze | solution.py:36
  1.9 0.5 %collective-permute-start.5 = (bf16[2,256,2304]{2,1,0:T(8,128)(2,1)S(1)}, bf16[2,256,2304]{2,1,0:T(8,128)(2,1)S(1)}, u32[]{:S(2)}, u32[]{:S(2)}) collective-permute-start(bf16[2,256,2304]{2,1,0:T(8,128)(2,1)S(1)} %slice_bitcast_fusion), channel_id=1, source_target_pairs={{0,1},{1,0},{2,3},{3,2},{4,5},{5,4},{6,7},{7,6},{8,9},{9,8},{10,11... | collective-permute-start | bytes 7077896 | tf_op jit(solution)/shard_map/ppermute | solution.py:10
  2.5 0.0 copy-done.1
  2.5 0.1 collective-permute-start.4
  2.6 0.0 copy-done.7
  2.6 0.1 fusion.20
  2.7 0.0 copy-done.6
  2.7 0.5 %collective-permute-start.3 = (f32[2,256]{1,0:T(2,128)S(1)}, f32[2,256]{1,0:T(2,128)S(1)}, u32[]{:S(2)}, u32[]{:S(2)}) collective-permute-start(f32[2,256]{1,0:T(2,128)S(1)} %pad_maximum_fusion.2), channel_id=1, source_target_pairs={{0,1},{1,0},{2,3},{3,2},{4,5},{5,4},{6,7},{7,6},{8,9},{9,8},{10,11... | collective-permute-start | bytes 6152 | tf_op jit(solution)/shard_map/ppermute | solution.py:10
  3.2 0.0 copy-done.2
  3.2 0.0 copy-done.3
  3.2 4.7 %collective-permute-start.2 = (bf16[2,14,2304]{2,1,0:T(8,128)(2,1)S(1)}, bf16[2,14,2304]{2,1,0:T(8,128)(2,1)S(1)}, u32[]{:S(2)}, u32[]{:S(2)}) collective-permute-start(bf16[2,14,2304]{2,1,0:T(8,128)(2,1)S(1)} %constant_dynamic-update-slice_fusion), channel_id=1, source_target_pairs={{0,12},{4,0},{8,4},{12,8},{1,13},{5,1},{9,5},{13,9},{2,14},{6,2},{... | collective-permute-start | bytes 387080 | tf_op jit(solution)/shard_map/ppermute | solution.py:10
  8.0 0.0 collective-permute-start.1
  8.0 0.4 collective-permute-done.3
  8.3 2.9 %collective-permute-start = (bf16[2,14,2304]{2,1,0:T(8,128)(2,1)S(1)}, bf16[2,14,2304]{2,1,0:T(8,128)(2,1)S(1)}, u32[]{:S(2)}, u32[]{:S(2)}) collective-permute-start(bf16[2,14,2304]{2,1,0:T(8,128)(2,1)S(1)} %constant_dynamic-update-slice_fusion), channel_id=1, source_target_pairs={{0,4},{4,8},{8,12},{12,0},{1,5},{5,9},{9,13},{13,1},{2,6},{6,10},{... | collective-permute-start | bytes 387080 | tf_op jit(solution)/shard_map/ppermute | solution.py:10
  11.3 0.9 %collective-permute-done.2 = bf16[2,14,2304]{2,1,0:T(8,128)(2,1)S(1)} collective-permute-done((bf16[2,14,2304]{2,1,0:T(8,128)(2,1)S(1)}, bf16[2,14,2304]{2,1,0:T(8,128)(2,1)S(1)}, u32[]{:S(2)}, u32[]{:S(2)}) %collective-permute-start.2) | collective-permute-done | bytes 129056 | tf_op jit(solution)/shard_map/ppermute | solution.py:10
  12.2 8.9 %collective-permute-done.1 = bf16[2,14,2304]{2,1,0:T(8,128)(2,1)S(1)} collective-permute-done((bf16[2,14,2304]{2,1,0:T(8,128)(2,1)S(1)}, bf16[2,14,2304]{2,1,0:T(8,128)(2,1)S(1)}, u32[]{:S(2)}, u32[]{:S(2)}) %collective-permute-start.1) | collective-permute-done | bytes 129056 | tf_op jit(solution)/shard_map/ppermute | solution.py:10
  21.1 0.0 collective-permute-done
  21.1 0.2 pad_maximum_fusion
  21.3 0.3 fusion.12
  21.6 0.0 copy-done.5
  21.6 0.0 slice-start
  21.6 0.0 copy-start
  21.6 0.3 fusion.9
  22.0 0.0 collective-permute-done.4
  22.0 0.3 fusion.11
  22.3 0.0 slice-done
  22.3 0.3 maximum_convert_fusion
  22.7 3.4 %collective-permute-start.6 = (bf16[56,512]{1,0:T(8,128)(2,1)S(1)}, bf16[56,512]{1,0:T(8,128)(2,1)S(1)}, u32[]{:S(2)}, u32[]{:S(2)}) collective-permute-start(bf16[56,512]{1,0:T(8,128)(2,1)S(1)} %pad_maximum_fusion.1), channel_id=1, source_target_pairs={{0,2},{1,3},{4,6},{5,7},{8,10},{9,11},{12,14},{13,15},{16,18},{17,... | collective-permute-start | bytes 172040 | tf_op jit(solution)/shard_map/ppermute | solution.py:10
  26.1 0.0 copy-done
  26.1 0.3 fusion.3
  26.4 1.5 %collective-permute-done.6 = bf16[56,512]{1,0:T(8,128)(2,1)S(1)} collective-permute-done((bf16[56,512]{1,0:T(8,128)(2,1)S(1)}, bf16[56,512]{1,0:T(8,128)(2,1)S(1)}, u32[]{:S(2)}, u32[]{:S(2)}) %collective-permute-start.6) | collective-permute-done | bytes 57376 | tf_op jit(solution)/shard_map/ppermute | solution.py:10
  27.9 0.0 collective-permute-done.5
  27.9 0.3 fusion.1
  28.2 0.3 convolution_add_fusion.1
  28.6 0.0 copy-start.4
  28.6 0.3 fusion.24
  29.0 0.1 fusion.23
  29.0 0.9 %collective-permute-start.9 = (bf16[14,2304]{1,0:T(8,128)(2,1)S(1)}, bf16[14,2304]{1,0:T(8,128)(2,1)S(1)}, u32[]{:S(2)}, u32[]{:S(2)}) collective-permute-start(bf16[14,2304]{1,0:T(8,128)(2,1)S(1)} %get-tuple-element.6), channel_id=1, source_target_pairs={{0,4},{4,8},{8,12},{12,0},{1,5},{5,9},{9,13},{13,1},{2,6},{6,10},{... | collective-permute-start | bytes 193544 | tf_op jit(solution)/shard_map/ppermute | solution.py:10
  29.9 2.0 %collective-permute-start.8 = (bf16[14,2304]{1,0:T(8,128)(2,1)S(1)}, bf16[14,2304]{1,0:T(8,128)(2,1)S(1)}, u32[]{:S(2)}, u32[]{:S(2)}) collective-permute-start(bf16[14,2304]{1,0:T(8,128)(2,1)S(1)} %get-tuple-element.7), channel_id=1, source_target_pairs={{0,8},{4,12},{8,0},{12,4},{1,9},{5,13},{9,1},{13,5},{2,10},{6,14},... | collective-permute-start | bytes 193544 | tf_op jit(solution)/shard_map/ppermute | solution.py:10
  31.9 2.8 %collective-permute-start.7 = (bf16[14,2304]{1,0:T(8,128)(2,1)S(1)}, bf16[14,2304]{1,0:T(8,128)(2,1)S(1)}, u32[]{:S(2)}, u32[]{:S(2)}) collective-permute-start(bf16[14,2304]{1,0:T(8,128)(2,1)S(1)} %get-tuple-element.5), channel_id=1, source_target_pairs={{0,12},{4,0},{8,4},{12,8},{1,13},{5,1},{9,5},{13,9},{2,14},{6,2},{... | collective-permute-start | bytes 193544 | tf_op jit(solution)/shard_map/ppermute | solution.py:10
  34.7 0.0 copy-done.4
  34.8 1.2 %collective-permute-done.9 = bf16[14,2304]{1,0:T(8,128)(2,1)S(1)} collective-permute-done((bf16[14,2304]{1,0:T(8,128)(2,1)S(1)}, bf16[14,2304]{1,0:T(8,128)(2,1)S(1)}, u32[]{:S(2)}, u32[]{:S(2)}) %collective-permute-start.9) | collective-permute-done | bytes 64544 | tf_op jit(solution)/shard_map/ppermute | solution.py:10
  35.9 1.5 %collective-permute-done.8 = bf16[14,2304]{1,0:T(8,128)(2,1)S(1)} collective-permute-done((bf16[14,2304]{1,0:T(8,128)(2,1)S(1)}, bf16[14,2304]{1,0:T(8,128)(2,1)S(1)}, u32[]{:S(2)}, u32[]{:S(2)}) %collective-permute-start.8) | collective-permute-done | bytes 64544 | tf_op jit(solution)/shard_map/ppermute | solution.py:10
  37.5 0.0 collective-permute-done.7
  37.5 0.7 %fusion.17 = bf16[1,14,2304]{2,1,0:T(8,128)(2,1)} fusion(bf16[14,2304]{1,0:T(8,128)(2,1)S(1)} %collective-permute-done.9, bf16[14,2304]{1,0:T(8,128)(2,1)S(1)} %collective-permute-done.8, bf16[14,2304]{1,0:T(8,128)(2,1)S(1)} %collective-permute-done.7, f32[56,2304]{1,0:T(8,128)S(1)} %get-tuple-element.11, f32[2304]{0:T(1024)S(1)} %reduce.1), kind=kLoop, calls=%fused_computation.27 | loop fusion | flops 258048 | bytes 396288 | tf_op jit(solution)/shard_map/broadcast_in_dim | solution.py:60
  (10 shorter events, 0.1 us)
Async XLA Ops:
  0.0 2.5 %copy-start.1 = (bf16[1,2304,256]{2,1,0:T(8,128)(2,1)S(1)}, bf16[1,2304,256]{2,1,0:T(8,128)(2,1)}, u32[]{:S(2)}) copy-start(bf16[1,2304,256]{2,1,0:T(8,128)(2,1)} %param.9) | copy-start | bytes 3538948
  0.0 2.6 %copy-start.7 = (s32[1,1,16]{2,1,0:T(1,128)S(1)}, s32[1,1,16]{2,1,0:T(1,128)}, u32[]{:S(2)}) copy-start(s32[1,1,16]{2,1,0:T(1,128)} %param.13) | copy-start | bytes 196
  0.0 2.7 %copy-start.6 = (f32[1,256]{1,0:T(1,128)S(1)}, f32[1,256]{1,0:T(1,128)}, u32[]{:S(2)}) copy-start(f32[1,256]{1,0:T(1,128)} %param.10) | copy-start | bytes 3076
  0.0 3.2 %copy-start.2 = (bf16[1,14,2304]{2,1,0:T(8,128)(2,1)S(1)}, bf16[1,14,2304]{2,1,0:T(8,128)(2,1)}, u32[]{:S(2)}) copy-start(bf16[1,14,2304]{2,1,0:T(8,128)(2,1)} %param.7) | copy-start | bytes 193540
  0.0 3.2 %copy-start.3 = (bf16[1,14,2304]{2,1,0:T(8,128)(2,1)S(1)}, bf16[1,14,2304]{2,1,0:T(8,128)(2,1)}, u32[]{:S(2)}) copy-start(bf16[1,14,2304]{2,1,0:T(8,128)(2,1)} %param.8) | copy-start | bytes 193540
  1.9 26.0 %collective-permute-start.5 = (bf16[2,256,2304]{2,1,0:T(8,128)(2,1)S(1)}, bf16[2,256,2304]{2,1,0:T(8,128)(2,1)S(1)}, u32[]{:S(2)}, u32[]{:S(2)}) collective-permute-start(bf16[2,256,2304]{2,1,0:T(8,128)(2,1)S(1)} %slice_bitcast_fusion), channel_id=1, source_target_pairs={{0,1},{1,0},{2,3},{3,2},{4,5},{5,4},{6,7},{7,6},{8,9},{9,8},{10,11... | collective-permute-start | bytes 7077896 | tf_op jit(solution)/shard_map/ppermute | solution.py:10
  2.5 19.5 %collective-permute-start.4 = (bf16[2304,256]{1,0:T(8,128)(2,1)S(1)}, bf16[2304,256]{1,0:T(8,128)(2,1)S(1)}, u32[]{:S(2)}, u32[]{:S(2)}) collective-permute-start(bf16[2304,256]{1,0:T(8,128)(2,1)S(1)} %bitcast.41), channel_id=1, source_target_pairs={{0,1},{1,0},{2,3},{3,2},{4,5},{5,4},{6,7},{7,6},{8,9},{9,8},{10,11... | collective-permute-start | bytes 3538952 | tf_op jit(solution)/shard_map/ppermute | solution.py:10
  2.7 5.6 %collective-permute-start.3 = (f32[2,256]{1,0:T(2,128)S(1)}, f32[2,256]{1,0:T(2,128)S(1)}, u32[]{:S(2)}, u32[]{:S(2)}) collective-permute-start(f32[2,256]{1,0:T(2,128)S(1)} %pad_maximum_fusion.2), channel_id=1, source_target_pairs={{0,1},{1,0},{2,3},{3,2},{4,5},{5,4},{6,7},{7,6},{8,9},{9,8},{10,11... | collective-permute-start | bytes 6152 | tf_op jit(solution)/shard_map/ppermute | solution.py:10
  3.2 8.9 %collective-permute-start.2 = (bf16[2,14,2304]{2,1,0:T(8,128)(2,1)S(1)}, bf16[2,14,2304]{2,1,0:T(8,128)(2,1)S(1)}, u32[]{:S(2)}, u32[]{:S(2)}) collective-permute-start(bf16[2,14,2304]{2,1,0:T(8,128)(2,1)S(1)} %constant_dynamic-update-slice_fusion), channel_id=1, source_target_pairs={{0,12},{4,0},{8,4},{12,8},{1,13},{5,1},{9,5},{13,9},{2,14},{6,2},{... | collective-permute-start | bytes 387080 | tf_op jit(solution)/shard_map/ppermute | solution.py:10
  8.0 13.1 %collective-permute-start.1 = (bf16[2,14,2304]{2,1,0:T(8,128)(2,1)S(1)}, bf16[2,14,2304]{2,1,0:T(8,128)(2,1)S(1)}, u32[]{:S(2)}, u32[]{:S(2)}) collective-permute-start(bf16[2,14,2304]{2,1,0:T(8,128)(2,1)S(1)} %constant_dynamic-update-slice_fusion), channel_id=1, source_target_pairs={{0,8},{4,12},{8,0},{12,4},{1,9},{5,13},{9,1},{13,5},{2,10},{6,14},... | collective-permute-start | bytes 387080 | tf_op jit(solution)/shard_map/ppermute | solution.py:10
  8.3 13.3 %copy-start.5 = (f32[2,256]{1,0:T(2,128)}, f32[2,256]{1,0:T(2,128)S(1)}, u32[]{:S(2)}) copy-start(f32[2,256]{1,0:T(2,128)S(1)} %collective-permute-done.3) | copy-start | bytes 6148
  8.3 12.8 %collective-permute-start = (bf16[2,14,2304]{2,1,0:T(8,128)(2,1)S(1)}, bf16[2,14,2304]{2,1,0:T(8,128)(2,1)S(1)}, u32[]{:S(2)}, u32[]{:S(2)}) collective-permute-start(bf16[2,14,2304]{2,1,0:T(8,128)(2,1)S(1)} %constant_dynamic-update-slice_fusion), channel_id=1, source_target_pairs={{0,4},{4,8},{8,12},{12,0},{1,5},{5,9},{9,13},{13,1},{2,6},{6,10},{... | collective-permute-start | bytes 387080 | tf_op jit(solution)/shard_map/ppermute | solution.py:10
  21.6 0.7 %slice-start = ((f32[2,256]{1,0:T(2,128)}), f32[1,256]{1,0:T(1,128)S(1)}, s32[]{:S(2)}) async-start(f32[2,256]{1,0:T(2,128)} %copy-done.5), calls=%async_computation | async-start | bytes 2048 | tf_op jit(solution)/shard_map/slice | solution.py:44
  21.6 4.5 %copy-start = (bf16[1,3,256,2304]{3,2,1,0:T(8,128)(2,1)S(1)}, bf16[1,3,256,2304]{3,2,1,0:T(8,128)(2,1)}, u32[]{:S(2)}) copy-start(bf16[1,3,256,2304]{3,2,1,0:T(8,128)(2,1)} %param.11) | copy-start | bytes 10616836
  22.7 5.2 %collective-permute-start.6 = (bf16[56,512]{1,0:T(8,128)(2,1)S(1)}, bf16[56,512]{1,0:T(8,128)(2,1)S(1)}, u32[]{:S(2)}, u32[]{:S(2)}) collective-permute-start(bf16[56,512]{1,0:T(8,128)(2,1)S(1)} %pad_maximum_fusion.1), channel_id=1, source_target_pairs={{0,2},{1,3},{4,6},{5,7},{8,10},{9,11},{12,14},{13,15},{16,18},{17,... | collective-permute-start | bytes 172040 | tf_op jit(solution)/shard_map/ppermute | solution.py:10
  28.6 6.2 %copy-start.4 = (f32[1,2304]{1,0:T(1,128)S(1)}, f32[1,2304]{1,0:T(1,128)}, u32[]{:S(2)}) copy-start(f32[1,2304]{1,0:T(1,128)} %param.12) | copy-start | bytes 27652
  29.0 6.9 %collective-permute-start.9 = (bf16[14,2304]{1,0:T(8,128)(2,1)S(1)}, bf16[14,2304]{1,0:T(8,128)(2,1)S(1)}, u32[]{:S(2)}, u32[]{:S(2)}) collective-permute-start(bf16[14,2304]{1,0:T(8,128)(2,1)S(1)} %get-tuple-element.6), channel_id=1, source_target_pairs={{0,4},{4,8},{8,12},{12,0},{1,5},{5,9},{9,13},{13,1},{2,6},{6,10},{... | collective-permute-start | bytes 193544 | tf_op jit(solution)/shard_map/ppermute | solution.py:10
  29.9 7.6 %collective-permute-start.8 = (bf16[14,2304]{1,0:T(8,128)(2,1)S(1)}, bf16[14,2304]{1,0:T(8,128)(2,1)S(1)}, u32[]{:S(2)}, u32[]{:S(2)}) collective-permute-start(bf16[14,2304]{1,0:T(8,128)(2,1)S(1)} %get-tuple-element.7), channel_id=1, source_target_pairs={{0,8},{4,12},{8,0},{12,4},{1,9},{5,13},{9,1},{13,5},{2,10},{6,14},... | collective-permute-start | bytes 193544 | tf_op jit(solution)/shard_map/ppermute | solution.py:10
  31.9 5.6 %collective-permute-start.7 = (bf16[14,2304]{1,0:T(8,128)(2,1)S(1)}, bf16[14,2304]{1,0:T(8,128)(2,1)S(1)}, u32[]{:S(2)}, u32[]{:S(2)}) collective-permute-start(bf16[14,2304]{1,0:T(8,128)(2,1)S(1)} %get-tuple-element.5), channel_id=1, source_target_pairs={{0,12},{4,0},{8,4},{12,8},{1,13},{5,1},{9,5},{13,9},{2,14},{6,2},{... | collective-permute-start | bytes 193544 | tf_op jit(solution)/shard_map/ppermute | solution.py:10

commit v2 on v1

v2 whole, which is shorter than its diff:
```python
import functools

import jax
import jax.numpy as jnp
from jax import lax
from jax.experimental import pallas as pl
from jax.experimental.pallas import tpu as pltpu
from jax.sharding import PartitionSpec as P

REACH = 3
SLOT = 16
FIRST = 0
VMEM = pltpu.VMEM
LIMIT = 48 * 1024 * 1024


def shifted(value, axis, by):
    count = lax.axis_size(axis)
    return lax.ppermute(value, axis, [(i, i + by) for i in range(count) if 0 <= i + by < count])


def rotated(value, axis, by):
    count = lax.axis_size(axis)
    return lax.ppermute(value, axis, [(i, (i + by) % count) for i in range(count)])


def near(value):
    return pltpu.with_memory_space_constraint(value, VMEM)


def far(value):
    return pltpu.with_memory_space_constraint(value, pltpu.HBM)


def call(body, outs, spaces, args, scratch=(), flops=0, moved=0):
    return pl.pallas_call(
        body,
        out_shape=outs,
        in_specs=[pl.BlockSpec(memory_space=s) for s in spaces],
        out_specs=jax.tree.map(lambda _: pl.BlockSpec(memory_space=VMEM), outs),
        scratch_shapes=list(scratch),
        compiler_params=pltpu.CompilerParams(vmem_limit_bytes=LIMIT),
        cost_estimate=pl.CostEstimate(flops=flops, bytes_accessed=moved, transcendentals=0),
    )(*args)


def stack_body(clean, corrupt, bias, picks, both, small, bias_v, picks_s, sems):
    copies = [
        pltpu.make_async_copy(picks.at[0], picks_s, sems.at[0]),
        pltpu.make_async_copy(bias, bias_v, sems.at[1]),
        pltpu.make_async_copy(clean.at[0], both.at[0], sems.at[2]),
        pltpu.make_async_copy(corrupt.at[0], both.at[1], sems.at[3]),
    ]
    for c in copies:
        c.start()
    copies[0].wait()
    width = small.shape[1]
    lane = lax.broadcasted_iota(jnp.int32, (1, width), 1)
    mark = jnp.zeros((1, width), jnp.float32)
    for i in range(picks_s.shape[1]):
        mark = jnp.where(lane == picks_s[0, i], 1.0, mark)
    small[1:2, :] = mark
    copies[1].wait()
    small[0:1, :] = bias_v[...]
    copies[2].wait()
    copies[3].wait()


def load_body(levels, enc, dec, after, enc_out, dec_out, sems):
    copies = [pltpu.make_async_copy(enc.at[0], enc_out, sems.at[0])]
    copies += [
        pltpu.make_async_copy(dec.at[0, k], dec_out.at[k], sems.at[k + 1]) for k in range(levels)
    ]
    for c in copies:
        c.start()
    for c in copies:
        c.wait()


def encode_body(chips, cores, *refs):
    got, smalls, encs = refs[:chips], refs[chips : chips + cores], refs[chips + cores : chips + 2 * cores]
    out, x = refs[chips + 2 * cores :]
    rows = got[0].shape[1]
    half = chips * SLOT
    for k in range(chips):
        for c in range(2):
            x[c * half + k * SLOT : c * half + k * SLOT + rows, :] = got[k][c]
    width = encs[0].shape[1]
    for j in range(cores):
        h = jnp.dot(x[...], encs[j][...], preferred_element_type=jnp.float32)
        pre = jnp.where(smalls[j][1:2, :] > 0.5, h[half:], h[:half]) + smalls[j][0:1, :]
        out[:, j * width : (j + 1) * width] = jnp.maximum(pre, 0.0).astype(jnp.bfloat16)


def dots(feats, decs, level, cores):
    width = decs[0].shape[1]
    total = None
    for j in range(cores):
        one = jnp.dot(
            feats[:, j * width : (j + 1) * width],
            decs[j][level],
            preferred_element_type=jnp.float32,
        )
        total = one if total is None else total + one
    return total


def own_body(cores, feats, *refs):
    decs, out = refs[:cores], refs[cores]
    out[...] = dots(feats, decs, 0, cores)


def rest_body(chips, cores, depth, rows, base, bias, *refs):
    known, decs = refs[:depth], refs[depth : depth + cores]
    outs = refs[depth + cores :]
    total = base[...]
    for k in range(depth):
        total = total + dots(known[k], decs, k + 1, cores)
    outs[0][...] = total[:rows] + bias[...]
    for k in range(1, chips):
        outs[k][...] = total[k * SLOT : k * SLOT + rows].astype(jnp.bfloat16)


def sum_body(own, *refs):
    total = own[...]
    for r in refs[:-1]:
        total = total + r[...].astype(jnp.float32)
    refs[-1][0] = total.astype(jnp.bfloat16)


def local(clean_resid, corrupt_resid, enc_weight, enc_bias, dec_weight, dec_bias, patch_index):
    chips = lax.axis_size("feat")
    cores = lax.axis_size("dec")
    depth = min(REACH - 1, lax.axis_size("layer") - 1)
    width = enc_weight.shape[2]
    rows, model = clean_resid.shape[1:]
    bf16, f32 = jnp.bfloat16, jnp.float32
    any_, hbm, dma = pl.ANY, pltpu.HBM, pltpu.SemaphoreType.DMA

    both, small = call(
        stack_body,
        (VMEM((2, rows, model), bf16), VMEM((2, width), f32)),
        (hbm,) * 4,
        [far(v) for v in (clean_resid, corrupt_resid, enc_bias, patch_index)],
        (VMEM((1, width), f32), pltpu.SMEM(patch_index.shape[1:], jnp.int32), dma((4,))),
    )
    got = [rotated(both, "feat", k) for k in range(chips - 1, 0, -1)]
    smalls = [small] + [rotated(small, "dec", j) for j in range(1, cores)]
    enc, dec = call(
        functools.partial(load_body, depth + 1),
        (VMEM((model, width), bf16), VMEM((depth + 1, width, model), bf16)),
        (hbm, hbm, any_),
        (far(enc_weight), far(dec_weight), smalls[-1]),
        (dma((depth + 2,)),),
    )
    got = [both] + got[::-1]
    encs = [enc] + [rotated(enc_weight[0], "dec", j) for j in range(1, cores)]
    decs = [dec] + [rotated(dec_weight[0], "dec", j) for j in range(1, cores)]
    feats = call(
        functools.partial(encode_body, chips, cores),
        VMEM((chips * SLOT, cores * width), bf16),
        (VMEM,) * (chips + 2 * cores),
        [near(v) for v in (*got, *smalls, *encs)],
        (VMEM((2 * chips * SLOT, model), bf16),),
        flops=4 * chips * SLOT * model * width * cores,
        moved=cores * width * model * 2,
    )
    known = [shifted(feats, "layer", o) for o in range(1, depth + 1)]
    base = call(
        functools.partial(own_body, cores),
        VMEM((chips * SLOT, model), f32),
        (VMEM,) * (1 + cores),
        [near(v) for v in (feats, *decs)],
        flops=2 * chips * SLOT * model * width * cores,
        moved=cores * width * model * 2,
    )
    parts = call(
        functools.partial(rest_body, chips, cores, depth, rows),
        (VMEM((rows, model), f32),) + (VMEM((rows, model), bf16),) * (chips - 1),
        (VMEM,) * (2 + depth + cores),
        [near(v) for v in (base, dec_bias, *known, *decs)],
        flops=2 * chips * SLOT * model * width * cores * depth,
        moved=cores * width * model * 2 * depth,
    )
    back = [rotated(parts[k], "feat", -k) for k in range(1, chips)]
    return call(
        sum_body,
        jax.ShapeDtypeStruct((1, rows, model), bf16),
        (VMEM,) * chips,
        [near(v) for v in (parts[0], *back)],
    )


def solution(mesh):
    placed = (
        P("layer", ("grp", "feat", "dec"), None),
        P("layer", ("grp", "feat", "dec"), None),
        P("layer", None, ("feat", "dec")),
        P("layer", ("feat", "dec")),
        P("layer", None, ("feat", "dec"), None),
        P("layer", None),
        P("layer", ("feat", "dec"), None),
    )
    return jax.shard_map(
        local,
        mesh=mesh,
        in_specs=placed,
        out_specs=P("layer", ("grp", "feat", "dec"), None),
        check_vma=False,
    )
```

time: 38.3 us -> 36 us (0.940)
  Pallas kernels: 0 us -> 5.23 us
  matrix products: 2.7 us -> 0 us
  local copies, waits for them, and re-layouts: 2.03 us -> 0.01 us
  starting transfers between devices: 17.9 us -> 16.4 us
  other arithmetic: 1.01 us -> 0 us
    pallas_call x0 -> x6, Pallas kernels: none -> 5.23 us  [call(): pl.pallas_call(body, out_shape=outs, in_specs=[pl.BlockSpec(memory_space=...]
    dot_general x8 -> x0, matrix products: 2.7 us -> none  [the longest x4 1.34 us: local(): jnp.dot(known[k][:, j * width:(j + 1) * width], decs[j][k], preferred_ele...]
    squeeze x1 -> x0, local copies, waits for them, and re-layouts: 1.92 us -> none  [local(): decw = dec_weight[0, :depth + 1]]
    ppermute x10, starting transfers between devices: 17.9 us -> 16.4 us  [the longest x9 13 us: rotated(): lax.ppermute(value, axis, [(i, (i + by) % count) for i in range(count)])]
    broadcast_in_dim x1 -> x0, other arithmetic: 0.68 us -> none  [local(): return (summed + dec_bias).astype(jnp.bfloat16)[None]]
  transfers between devices with their start and end apart: 10 -> 10, of which waited for: 6 -> 4; matrix products, arithmetic and copies ran while one was open for 5% -> 0% of each run, Pallas kernels for 0% -> 11%
where the time goes in v2:
time: 36 us; the launch traced here: 35.8 us
  starting transfers between devices  16.4 us (46%)
  waiting for transfers between devices  14.1 us (39%)
  Pallas kernels  5.23 us (15%)
    ppermute x9, starting transfers between devices, rotated(): lax.ppermute(value, axis, [(i, (i + by) % count) for i in range(count)])  13 us
    ppermute x9, waiting for transfers between devices, rotated(): lax.ppermute(value, axis, [(i, (i + by) % count) for i in range(count)])  12.8 us
    pallas_call x6, Pallas kernels, call(): pl.pallas_call(body, out_shape=outs, in_specs=[pl.BlockSpec(memory_space=...  5.23 us
    ppermute x1, starting transfers between devices, shifted(): lax.ppermute(value, axis, [(i, i + by) for i in range(count) if 0 <= i +...  3.39 us
    ppermute x1, waiting for transfers between devices, shifted(): lax.ppermute(value, axis, [(i, i + by) for i in range(count) if 0 <= i +...  1.33 us
  transfers between devices with their start and end apart: 10, of which 4 were waited for; matrix products, arithmetic and copies ran while one was open for 0% of the time, Pallas kernels for 11%

profile of v2, /device:TPU:0, one launch (start us, length us, event | category | flops | bytes accessed | tf_op | source)
XLA Modules:
  0.0 35.8 jit_solution(6178506313363445532)
XLA Ops:
  0.0 0.5 %collective-permute-start.5 = (bf16[3,256,2304]{2,1,0:T(8,128)(2,1)}, bf16[3,256,2304]{2,1,0:T(8,128)(2,1)S(1)}, u32[]{:S(2)}, u32[]{:S(2)}) collective-permute-start(bf16[3,256,2304]{2,1,0:T(8,128)(2,1)} %bitcast.2), channel_id=1, source_target_pairs={{0,1},{1,0},{2,3},{3,2},{4,5},{5,4},{6,7},{7,6},{8,9},{9,8},{10,11... | collective-permute-start | bytes 10616840 | tf_op jit(solution)/shard_map/ppermute | solution.py:24
  0.5 0.1 collective-permute-start.4
  0.5 1.0 %shard_map.73 = (bf16[2,14,2304]{2,1,0:T(8,128)(2,1)S(1)}, f32[2,256]{1,0:T(2,128)S(1)}) custom-call(bf16[1,14,2304]{2,1,0:T(8,128)(2,1)} %clean.1, bf16[1,14,2304]{2,1,0:T(8,128)(2,1)} %corrupt.1, f32[1,256]{1,0:T(1,128)} %bias.2, s32[1,1,16]{2,1,0:T(1,128)} %picks.1), custom_call_target="tpu_custom_call" | custom-call | tf_op jit(solution)/shard_map/pallas_call | solution.py:36
  1.5 0.5 %collective-permute-start.3 = (f32[2,256]{1,0:T(2,128)S(1)}, f32[2,256]{1,0:T(2,128)S(1)}, u32[]{:S(2)}, u32[]{:S(2)}) collective-permute-start(f32[2,256]{1,0:T(2,128)S(1)} %get-tuple-element.14.refs_4_), channel_id=1, source_target_pairs={{0,1},{1,0},{2,3},{3,2},{4,5},{5,4},{6,7},{7,6},{8,9},{9,8},{10,11... | collective-permute-start | bytes 6152 | tf_op jit(solution)/shard_map/ppermute | solution.py:24
  2.0 4.7 %collective-permute-start.2 = (bf16[2,14,2304]{2,1,0:T(8,128)(2,1)S(1)}, bf16[2,14,2304]{2,1,0:T(8,128)(2,1)S(1)}, u32[]{:S(2)}, u32[]{:S(2)}) collective-permute-start(bf16[2,14,2304]{2,1,0:T(8,128)(2,1)S(1)} %get-tuple-element.13.refs_0_), channel_id=1, source_target_pairs={{0,12},{4,0},{8,4},{12,8},{1,13},{5,1},{9,5},{13,9},{2,14},{6,2},{... | collective-permute-start | bytes 387080 | tf_op jit(solution)/shard_map/ppermute | solution.py:24
  6.7 0.0 collective-permute-start.1
  6.7 0.0 collective-permute-done.3.after.refs_5_
  6.7 2.6 %collective-permute-start = (bf16[2,14,2304]{2,1,0:T(8,128)(2,1)S(1)}, bf16[2,14,2304]{2,1,0:T(8,128)(2,1)S(1)}, u32[]{:S(2)}, u32[]{:S(2)}) collective-permute-start(bf16[2,14,2304]{2,1,0:T(8,128)(2,1)S(1)} %get-tuple-element.13.refs_0_), channel_id=1, source_target_pairs={{0,4},{4,8},{8,12},{12,0},{1,5},{5,9},{9,13},{13,1},{2,6},{6,10},{... | collective-permute-start | bytes 387080 | tf_op jit(solution)/shard_map/ppermute | solution.py:24
  9.2 2.0 %shard_map.74 = (bf16[2304,256]{1,0:T(8,128)(2,1)S(1)}, bf16[2,256,2304]{2,1,0:T(8,128)(2,1)S(1)}) custom-call(bf16[1,2304,256]{2,1,0:T(8,128)(2,1)} %enc.1, bf16[1,3,256,2304]{3,2,1,0:T(8,128)(2,1)} %dec.1, f32[2,256]{1,0:T(2,128)S(1)} %collective-permute-done.3.after.refs_5_), custom_call_target="tpu_custom_call" | custom-call | tf_op jit(solution)/shard_map/pallas_call | solution.py:36
  11.3 0.0 collective-permute-done.2.refs_3_
  11.3 8.5 %collective-permute-done.1.refs_2_ = bf16[2,14,2304]{2,1,0:T(8,128)(2,1)S(1)} collective-permute-done((bf16[2,14,2304]{2,1,0:T(8,128)(2,1)S(1)}, bf16[2,14,2304]{2,1,0:T(8,128)(2,1)S(1)}, u32[]{:S(2)}, u32[]{:S(2)}) %collective-permute-start.1) | collective-permute-done | bytes 129056 | tf_op jit(solution)/shard_map/ppermute | solution.py:24
  19.8 0.0 collective-permute-done.refs_1_
  19.8 0.0 collective-permute-done.4.refs_7_
  19.8 0.5 %shard_map.75.feats = bf16[64,512]{1,0:T(8,128)(2,1)S(1)} custom-call(bf16[2,14,2304]{2,1,0:T(8,128)(2,1)S(1)} %get-tuple-element.13.refs_0_, bf16[2,14,2304]{2,1,0:T(8,128)(2,1)S(1)} %collective-permute-done.refs_1_, bf16[2,14,2304]{2,1,0:T(8,128)(2,1)S(1)} %collective-permute-done.1.refs_2_, bf16[2,14,2304]{2,1,0:T(8,128)(2,1)S(1)} %collective-permute-done.2.refs_3_, ...), custom_call_target="tpu_custom_call" | custom-call | flops 301989888 | bytes 2359296 | tf_op jit(solution)/shard_map/pallas_call | solution.py:36
  20.3 3.4 %collective-permute-start.6 = (bf16[64,512]{1,0:T(8,128)(2,1)S(1)}, bf16[64,512]{1,0:T(8,128)(2,1)S(1)}, u32[]{:S(2)}, u32[]{:S(2)}) collective-permute-start(bf16[64,512]{1,0:T(8,128)(2,1)S(1)} %shard_map.75.feats), channel_id=1, source_target_pairs={{0,2},{1,3},{4,6},{5,7},{8,10},{9,11},{12,14},{13,15},{16,18},{17,... | collective-permute-start | bytes 196616 | tf_op jit(solution)/shard_map/ppermute | solution.py:19
  23.7 0.0 collective-permute-done.5.refs_1_.refs_2_
  23.7 0.0 copy-start
  23.8 0.5 %shard_map.76.base = f32[64,2304]{1,0:T(8,128)S(1)} custom-call(bf16[64,512]{1,0:T(8,128)(2,1)S(1)} %shard_map.75.feats, bf16[2,256,2304]{2,1,0:T(8,128)(2,1)S(1)} %get-tuple-element.16.refs_0_.refs_1_, bf16[3,256,2304]{2,1,0:T(8,128)(2,1)S(1)} %collective-permute-done.5.refs_1_.refs_2_), custom_call_target="tpu_custom_call" | custom-call | flops 150994944 | bytes 2359296 | tf_op jit(solution)/shard_map/pallas_call | solution.py:36
  24.3 1.3 %collective-permute-done.6.refs_0_ = bf16[64,512]{1,0:T(8,128)(2,1)S(1)} collective-permute-done((bf16[64,512]{1,0:T(8,128)(2,1)S(1)}, bf16[64,512]{1,0:T(8,128)(2,1)S(1)}, u32[]{:S(2)}, u32[]{:S(2)}) %collective-permute-start.6) | collective-permute-done | bytes 65568 | tf_op jit(solution)/shard_map/ppermute | solution.py:19
  25.6 0.0 copy-done
  25.6 0.5 %shard_map.77 = (f32[14,2304]{1,0:T(8,128)S(1)}, bf16[14,2304]{1,0:T(8,128)(2,1)S(1)}, bf16[14,2304]{1,0:T(8,128)(2,1)S(1)}, bf16[14,2304]{1,0:T(8,128)(2,1)S(1)}) custom-call(f32[64,2304]{1,0:T(8,128)S(1)} %shard_map.76.base, f32[1,2304]{1,0:T(1,128)S(1)} %copy-done, bf16[64,512]{1,0:T(8,128)(2,1)S(1)} %collective-permute-done.6.refs_0_, ...), custom_call_target="tpu_custom_call" | custom-call | flops 150994944 | bytes 2359296 | tf_op jit(solution)/shard_map/pallas_call | solution.py:36
  26.2 1.3 %collective-permute-start.7 = (bf16[14,2304]{1,0:T(8,128)(2,1)S(1)}, bf16[14,2304]{1,0:T(8,128)(2,1)S(1)}, u32[]{:S(2)}, u32[]{:S(2)}) collective-permute-start(bf16[14,2304]{1,0:T(8,128)(2,1)S(1)} %get-tuple-element.18), channel_id=1, source_target_pairs={{0,12},{4,0},{8,4},{12,8},{1,13},{5,1},{9,5},{13,9},{2,14},{6,2},{... | collective-permute-start | bytes 193544 | tf_op jit(solution)/shard_map/ppermute | solution.py:24
  27.4 1.6 %collective-permute-start.8 = (bf16[14,2304]{1,0:T(8,128)(2,1)S(1)}, bf16[14,2304]{1,0:T(8,128)(2,1)S(1)}, u32[]{:S(2)}, u32[]{:S(2)}) collective-permute-start(bf16[14,2304]{1,0:T(8,128)(2,1)S(1)} %get-tuple-element.19), channel_id=1, source_target_pairs={{0,8},{4,12},{8,0},{12,4},{1,9},{5,13},{9,1},{13,5},{2,10},{6,14},... | collective-permute-start | bytes 193544 | tf_op jit(solution)/shard_map/ppermute | solution.py:24
  29.0 1.9 %collective-permute-start.9 = (bf16[14,2304]{1,0:T(8,128)(2,1)S(1)}, bf16[14,2304]{1,0:T(8,128)(2,1)S(1)}, u32[]{:S(2)}, u32[]{:S(2)}) collective-permute-start(bf16[14,2304]{1,0:T(8,128)(2,1)S(1)} %get-tuple-element.20), channel_id=1, source_target_pairs={{0,4},{4,8},{8,12},{12,0},{1,5},{5,9},{9,13},{13,1},{2,6},{6,10},{... | collective-permute-start | bytes 193544 | tf_op jit(solution)/shard_map/ppermute | solution.py:24
  30.9 0.0 collective-permute-done.7.refs_0_
  30.9 3.2 %collective-permute-done.8.refs_1_ = bf16[14,2304]{1,0:T(8,128)(2,1)S(1)} collective-permute-done((bf16[14,2304]{1,0:T(8,128)(2,1)S(1)}, bf16[14,2304]{1,0:T(8,128)(2,1)S(1)}, u32[]{:S(2)}, u32[]{:S(2)}) %collective-permute-start.8) | collective-permute-done | bytes 64544 | tf_op jit(solution)/shard_map/ppermute | solution.py:24
  34.2 1.0 %collective-permute-done.9.refs_2_ = bf16[14,2304]{1,0:T(8,128)(2,1)S(1)} collective-permute-done((bf16[14,2304]{1,0:T(8,128)(2,1)S(1)}, bf16[14,2304]{1,0:T(8,128)(2,1)S(1)}, u32[]{:S(2)}, u32[]{:S(2)}) %collective-permute-start.9) | collective-permute-done | bytes 64544 | tf_op jit(solution)/shard_map/ppermute | solution.py:24
  35.2 0.7 %shard_map.78 = bf16[1,14,2304]{2,1,0:T(8,128)(2,1)} custom-call(f32[14,2304]{1,0:T(8,128)S(1)} %get-tuple-element.17.own, bf16[14,2304]{1,0:T(8,128)(2,1)S(1)} %collective-permute-done.7.refs_0_, bf16[14,2304]{1,0:T(8,128)(2,1)S(1)} %collective-permute-done.8.refs_1_, bf16[14,2304]{1,0:T(8,128)(2,1)S(1)} %collective-permute-done.9.refs_2_), custom_call_target="tpu_custom_call" | custom-call | tf_op jit(solution)/shard_map/pallas_call | solution.py:36
Async XLA Ops:
  0.0 23.7 %collective-permute-start.5 = (bf16[3,256,2304]{2,1,0:T(8,128)(2,1)}, bf16[3,256,2304]{2,1,0:T(8,128)(2,1)S(1)}, u32[]{:S(2)}, u32[]{:S(2)}) collective-permute-start(bf16[3,256,2304]{2,1,0:T(8,128)(2,1)} %bitcast.2), channel_id=1, source_target_pairs={{0,1},{1,0},{2,3},{3,2},{4,5},{5,4},{6,7},{7,6},{8,9},{9,8},{10,11... | collective-permute-start | bytes 10616840 | tf_op jit(solution)/shard_map/ppermute | solution.py:24
  0.5 19.4 %collective-permute-start.4 = (bf16[2304,256]{1,0:T(8,128)(2,1)}, bf16[2304,256]{1,0:T(8,128)(2,1)S(1)}, u32[]{:S(2)}, u32[]{:S(2)}) collective-permute-start(bf16[2304,256]{1,0:T(8,128)(2,1)} %bitcast.3), channel_id=1, source_target_pairs={{0,1},{1,0},{2,3},{3,2},{4,5},{5,4},{6,7},{7,6},{8,9},{9,8},{10,11... | collective-permute-start | bytes 3538952 | tf_op jit(solution)/shard_map/ppermute | solution.py:24
  1.5 5.2 %collective-permute-start.3 = (f32[2,256]{1,0:T(2,128)S(1)}, f32[2,256]{1,0:T(2,128)S(1)}, u32[]{:S(2)}, u32[]{:S(2)}) collective-permute-start(f32[2,256]{1,0:T(2,128)S(1)} %get-tuple-element.14.refs_4_), channel_id=1, source_target_pairs={{0,1},{1,0},{2,3},{3,2},{4,5},{5,4},{6,7},{7,6},{8,9},{9,8},{10,11... | collective-permute-start | bytes 6152 | tf_op jit(solution)/shard_map/ppermute | solution.py:24
  2.0 9.3 %collective-permute-start.2 = (bf16[2,14,2304]{2,1,0:T(8,128)(2,1)S(1)}, bf16[2,14,2304]{2,1,0:T(8,128)(2,1)S(1)}, u32[]{:S(2)}, u32[]{:S(2)}) collective-permute-start(bf16[2,14,2304]{2,1,0:T(8,128)(2,1)S(1)} %get-tuple-element.13.refs_0_), channel_id=1, source_target_pairs={{0,12},{4,0},{8,4},{12,8},{1,13},{5,1},{9,5},{13,9},{2,14},{6,2},{... | collective-permute-start | bytes 387080 | tf_op jit(solution)/shard_map/ppermute | solution.py:24
  6.7 13.1 %collective-permute-start.1 = (bf16[2,14,2304]{2,1,0:T(8,128)(2,1)S(1)}, bf16[2,14,2304]{2,1,0:T(8,128)(2,1)S(1)}, u32[]{:S(2)}, u32[]{:S(2)}) collective-permute-start(bf16[2,14,2304]{2,1,0:T(8,128)(2,1)S(1)} %get-tuple-element.13.refs_0_), channel_id=1, source_target_pairs={{0,8},{4,12},{8,0},{12,4},{1,9},{5,13},{9,1},{13,5},{2,10},{6,14},... | collective-permute-start | bytes 387080 | tf_op jit(solution)/shard_map/ppermute | solution.py:24
  6.7 13.1 %collective-permute-start = (bf16[2,14,2304]{2,1,0:T(8,128)(2,1)S(1)}, bf16[2,14,2304]{2,1,0:T(8,128)(2,1)S(1)}, u32[]{:S(2)}, u32[]{:S(2)}) collective-permute-start(bf16[2,14,2304]{2,1,0:T(8,128)(2,1)S(1)} %get-tuple-element.13.refs_0_), channel_id=1, source_target_pairs={{0,4},{4,8},{8,12},{12,0},{1,5},{5,9},{9,13},{13,1},{2,6},{6,10},{... | collective-permute-start | bytes 387080 | tf_op jit(solution)/shard_map/ppermute | solution.py:24
  20.3 5.3 %collective-permute-start.6 = (bf16[64,512]{1,0:T(8,128)(2,1)S(1)}, bf16[64,512]{1,0:T(8,128)(2,1)S(1)}, u32[]{:S(2)}, u32[]{:S(2)}) collective-permute-start(bf16[64,512]{1,0:T(8,128)(2,1)S(1)} %shard_map.75.feats), channel_id=1, source_target_pairs={{0,2},{1,3},{4,6},{5,7},{8,10},{9,11},{12,14},{13,15},{16,18},{17,... | collective-permute-start | bytes 196616 | tf_op jit(solution)/shard_map/ppermute | solution.py:19
  23.7 1.9 %copy-start = (f32[1,2304]{1,0:T(1,128)S(1)}, f32[1,2304]{1,0:T(1,128)}, u32[]{:S(2)}) copy-start(f32[1,2304]{1,0:T(1,128)} %bias.3) | copy-start | bytes 27652
  26.2 4.8 %collective-permute-start.7 = (bf16[14,2304]{1,0:T(8,128)(2,1)S(1)}, bf16[14,2304]{1,0:T(8,128)(2,1)S(1)}, u32[]{:S(2)}, u32[]{:S(2)}) collective-permute-start(bf16[14,2304]{1,0:T(8,128)(2,1)S(1)} %get-tuple-element.18), channel_id=1, source_target_pairs={{0,12},{4,0},{8,4},{12,8},{1,13},{5,1},{9,5},{13,9},{2,14},{6,2},{... | collective-permute-start | bytes 193544 | tf_op jit(solution)/shard_map/ppermute | solution.py:24
  27.4 6.8 %collective-permute-start.8 = (bf16[14,2304]{1,0:T(8,128)(2,1)S(1)}, bf16[14,2304]{1,0:T(8,128)(2,1)S(1)}, u32[]{:S(2)}, u32[]{:S(2)}) collective-permute-start(bf16[14,2304]{1,0:T(8,128)(2,1)S(1)} %get-tuple-element.19), channel_id=1, source_target_pairs={{0,8},{4,12},{8,0},{12,4},{1,9},{5,13},{9,1},{13,5},{2,10},{6,14},... | collective-permute-start | bytes 193544 | tf_op jit(solution)/shard_map/ppermute | solution.py:24
  29.0 6.2 %collective-permute-start.9 = (bf16[14,2304]{1,0:T(8,128)(2,1)S(1)}, bf16[14,2304]{1,0:T(8,128)(2,1)S(1)}, u32[]{:S(2)}, u32[]{:S(2)}) collective-permute-start(bf16[14,2304]{1,0:T(8,128)(2,1)S(1)} %get-tuple-element.20), channel_id=1, source_target_pairs={{0,4},{4,8},{8,12},{12,0},{1,5},{5,9},{9,13},{13,1},{2,6},{6,10},{... | collective-permute-start | bytes 193544 | tf_op jit(solution)/shard_map/ppermute | solution.py:24

commit v3 on v2

--- a/solution.py
+++ b/solution.py
@@ -44,12 +44,25 @@
     )(*args)
 
 
-def stack_body(clean, corrupt, bias, picks, both, small, bias_v, picks_s, sems):
+def stack_body(clean, corrupt, both, sems):
+    copies = [
+        pltpu.make_async_copy(clean.at[0], both.at[0], sems.at[0]),
+        pltpu.make_async_copy(corrupt.at[0], both.at[1], sems.at[1]),
+    ]
+    for c in copies:
+        c.start()
+    for c in copies:
+        c.wait()
+
+
+def load_body(levels, enc, dec, bias, picks, after, enc_out, dec_out, small, bias_v, picks_s, sems):
     copies = [
         pltpu.make_async_copy(picks.at[0], picks_s, sems.at[0]),
         pltpu.make_async_copy(bias, bias_v, sems.at[1]),
-        pltpu.make_async_copy(clean.at[0], both.at[0], sems.at[2]),
-        pltpu.make_async_copy(corrupt.at[0], both.at[1], sems.at[3]),
+        pltpu.make_async_copy(enc.at[0], enc_out, sems.at[2]),
+    ]
+    copies += [
+        pltpu.make_async_copy(dec.at[0, k], dec_out.at[k], sems.at[k + 3]) for k in range(levels)
     ]
     for c in copies:
         c.start()
@@ -62,23 +75,12 @@
     small[1:2, :] = mark
     copies[1].wait()
     small[0:1, :] = bias_v[...]
-    copies[2].wait()
-    copies[3].wait()
-
-
-def load_body(levels, enc, dec, after, enc_out, dec_out, sems):
-    copies = [pltpu.make_async_copy(enc.at[0], enc_out, sems.at[0])]
-    copies += [
-        pltpu.make_async_copy(dec.at[0, k], dec_out.at[k], sems.at[k + 1]) for k in range(levels)
-    ]
-    for c in copies:
-        c.start()
-    for c in copies:
+    for c in copies[2:]:
         c.wait()
 
 
 def encode_body(chips, cores, *refs):
-    got, smalls, encs = refs[:chips], refs[chips : chips + cores], refs[chips + cores : chips + 2 * cores]
+    got, smalls, encs = refs[:chips][::-1], refs[chips : chips + cores], refs[chips + cores : chips + 2 * cores]
     out, x = refs[chips + 2 * cores :]
     rows = got[0].shape[1]
     half = chips * SLOT
@@ -113,9 +115,14 @@
 def rest_body(chips, cores, depth, rows, base, bias, *refs):
     known, decs = refs[:depth], refs[depth : depth + cores]
     outs = refs[depth + cores :]
-    total = base[...]
+    outs, total = outs[:-1], outs[-1]
+    total[...] = base[...]
     for k in range(depth):
-        total = total + dots(known[k], decs, k + 1, cores)
+
+        @pl.when(lax.axis_index("layer") > k)
+        def _():
+            total[...] += dots(known[k], decs, k + 1, cores)
+
     outs[0][...] = total[:rows] + bias[...]
     for k in range(1, chips):
         outs[k][...] = total[k * SLOT : k * SLOT + rows].astype(jnp.bfloat16)
@@ -137,35 +144,43 @@
     bf16, f32 = jnp.bfloat16, jnp.float32
     any_, hbm, dma = pl.ANY, pltpu.HBM, pltpu.SemaphoreType.DMA
 
-    both, small = call(
+    both = call(
         stack_body,
-        (VMEM((2, rows, model), bf16), VMEM((2, width), f32)),
-        (hbm,) * 4,
-        [far(v) for v in (clean_resid, corrupt_resid, enc_bias, patch_index)],
-        (VMEM((1, width), f32), pltpu.SMEM(patch_index.shape[1:], jnp.int32), dma((4,))),
-    )
-    got = [rotated(both, "feat", k) for k in range(chips - 1, 0, -1)]
+        VMEM((2, rows, model), bf16),
+        (hbm,) * 2,
+        [far(v) for v in (clean_resid, corrupt_resid)],
+        (dma((2,)),),
+    )
+    got = [rotated(both, "feat", k) for k in range(1, chips)]
+    enc, dec, small = call(
+        functools.partial(load_body, depth + 1),
+        (
+            VMEM((model, width), bf16),
+            VMEM((depth + 1, width, model), bf16),
+            VMEM((2, width), f32),
+        ),
+        (hbm,) * 4 + (any_,),
+        [far(v) for v in (enc_weight, dec_weight, enc_bias, patch_index)] + [got[2]],
+        (
+            VMEM((1, width), f32),
+            pltpu.SMEM(patch_index.shape[1:], jnp.int32),
+            dma((depth + 4,)),
+        ),
+    )
     smalls = [small] + [rotated(small, "dec", j) for j in range(1, cores)]
-    enc, dec = call(
-        functools.partial(load_body, depth + 1),
-        (VMEM((model, width), bf16), VMEM((depth + 1, width, model), bf16)),
-        (hbm, hbm, any_),
-        (far(enc_weight), far(dec_weight), smalls[-1]),
-        (dma((depth + 2,)),),
-    )
-    got = [both] + got[::-1]
+    got = [both] + got
     encs = [enc] + [rotated(enc_weight[0], "dec", j) for j in range(1, cores)]
     decs = [dec] + [rotated(dec_weight[0], "dec", j) for j in range(1, cores)]
     feats = call(
         functools.partial(encode_body, chips, cores),
         VMEM((chips * SLOT, cores * width), bf16),
         (VMEM,) * (chips + 2 * cores),
-        [near(v) for v in (*got, *smalls, *encs)],
+        [near(v) for v in (*got[::-1], *smalls, *encs)],
         (VMEM((2 * chips * SLOT, model), bf16),),
         flops=4 * chips * SLOT * model * width * cores,
         moved=cores * width * model * 2,
     )
-    known = [shifted(feats, "layer", o) for o in range(1, depth + 1)]
+    known = [rotated(feats, "layer", o) for o in range(1, depth + 1)]
     base = call(
         functools.partial(own_body, cores),
         VMEM((chips * SLOT, model), f32),
@@ -179,10 +194,11 @@
         (VMEM((rows, model), f32),) + (VMEM((rows, model), bf16),) * (chips - 1),
         (VMEM,) * (2 + depth + cores),
         [near(v) for v in (base, dec_bias, *known, *decs)],
+        (VMEM((chips * SLOT, model), f32),),
         flops=2 * chips * SLOT * model * width * cores * depth,
         moved=cores * width * model * 2 * depth,
     )
-    back = [rotated(parts[k], "feat", -k) for k in range(1, chips)]
+    back = [rotated(parts[k], "feat", -k) for k in range(chips - 1, 0, -1)]
     return call(
         sum_body,
         jax.ShapeDtypeStruct((1, rows, model), bf16),

time: 36 us -> 32.6 us (0.906)
  starting transfers between devices: 16.4 us -> 12.1 us
  waiting for transfers between devices: 14.1 us -> 15.5 us
  Pallas kernels: 5.23 us -> 4.77 us
    ppermute x1 -> x0, starting transfers between devices: 3.39 us -> none  [shifted(): lax.ppermute(value, axis, [(i, i + by) for i in range(count) if 0 <= i +...]
    ppermute x9 -> x10, waiting for transfers between devices: 12.8 us -> 15.5 us  [rotated(): lax.ppermute(value, axis, [(i, (i + by) % count) for i in range(count)])]
    ppermute x1 -> x0, waiting for transfers between devices: 1.33 us -> none  [shifted(): lax.ppermute(value, axis, [(i, i + by) for i in range(count) if 0 <= i +...]
    ppermute x9 -> x10, starting transfers between devices: 13 us -> 12.1 us  [rotated(): lax.ppermute(value, axis, [(i, (i + by) % count) for i in range(count)])]
    pallas_call x6, Pallas kernels: 5.23 us -> 4.77 us  [call(): pl.pallas_call(body, out_shape=outs, in_specs=[pl.BlockSpec(memory_space=...]
  transfers between devices with their start and end apart: 10 -> 10, of which waited for: 4 -> 7; matrix products, arithmetic and copies ran while one was open for 0% -> 0% of each run, Pallas kernels for 11% -> 12%
where the time goes in v3:
time: 32.6 us; the launch traced here: 32.5 us
  waiting for transfers between devices  15.5 us (48%)
  starting transfers between devices  12.1 us (37%)
  Pallas kernels  4.77 us (15%)
    ppermute x10, waiting for transfers between devices, rotated(): lax.ppermute(value, axis, [(i, (i + by) % count) for i in range(count)])  15.5 us
    ppermute x10, starting transfers between devices, rotated(): lax.ppermute(value, axis, [(i, (i + by) % count) for i in range(count)])  12.1 us
    pallas_call x6, Pallas kernels, call(): pl.pallas_call(body, out_shape=outs, in_specs=[pl.BlockSpec(memory_space=...  4.77 us
  transfers between devices with their start and end apart: 10, of which 7 were waited for; matrix products, arithmetic and copies ran while one was open for 0% of the time, Pallas kernels for 12%

profile of v3, /device:TPU:0, one launch (start us, length us, event | category | flops | bytes accessed | tf_op | source)
XLA Modules:
  0.0 32.5 jit_solution(18076378813600238736)
XLA Ops:
  0.0 0.5 %collective-permute-start.5 = (bf16[3,256,2304]{2,1,0:T(8,128)(2,1)}, bf16[3,256,2304]{2,1,0:T(8,128)(2,1)S(1)}, u32[]{:S(2)}, u32[]{:S(2)}) collective-permute-start(bf16[3,256,2304]{2,1,0:T(8,128)(2,1)} %bitcast.2), channel_id=1, source_target_pairs={{0,1},{1,0},{2,3},{3,2},{4,5},{5,4},{6,7},{7,6},{8,9},{9,8},{10,11... | collective-permute-start | bytes 10616840 | tf_op jit(solution)/shard_map/ppermute | solution.py:24
  0.5 0.1 collective-permute-start.4
  0.5 0.9 %shard_map.73.refs_3_ = bf16[2,14,2304]{2,1,0:T(8,128)(2,1)S(1)} custom-call(bf16[1,14,2304]{2,1,0:T(8,128)(2,1)} %clean.1, bf16[1,14,2304]{2,1,0:T(8,128)(2,1)} %corrupt.1), custom_call_target="tpu_custom_call" | custom-call | tf_op jit(solution)/shard_map/pallas_call | solution.py:36
  1.5 5.1 %collective-permute-start = (bf16[2,14,2304]{2,1,0:T(8,128)(2,1)S(1)}, bf16[2,14,2304]{2,1,0:T(8,128)(2,1)S(1)}, u32[]{:S(2)}, u32[]{:S(2)}) collective-permute-start(bf16[2,14,2304]{2,1,0:T(8,128)(2,1)S(1)} %shard_map.73.refs_3_), channel_id=1, source_target_pairs={{0,12},{4,0},{8,4},{12,8},{1,13},{5,1},{9,5},{13,9},{2,14},{6,2},{... | collective-permute-start | bytes 387080 | tf_op jit(solution)/shard_map/ppermute | solution.py:24
  6.6 0.0 collective-permute-start.2
  6.6 1.0 %collective-permute-start.1 = (bf16[2,14,2304]{2,1,0:T(8,128)(2,1)S(1)}, bf16[2,14,2304]{2,1,0:T(8,128)(2,1)S(1)}, u32[]{:S(2)}, u32[]{:S(2)}) collective-permute-start(bf16[2,14,2304]{2,1,0:T(8,128)(2,1)S(1)} %shard_map.73.refs_3_), channel_id=1, source_target_pairs={{0,8},{4,12},{8,0},{12,4},{1,9},{5,13},{9,1},{13,5},{2,10},{6,14},... | collective-permute-start | bytes 387080 | tf_op jit(solution)/shard_map/ppermute | solution.py:24
  7.6 3.3 %collective-permute-done.after.refs_0_ = bf16[2,14,2304]{2,1,0:T(8,128)(2,1)S(1)} collective-permute-done((bf16[2,14,2304]{2,1,0:T(8,128)(2,1)S(1)}, bf16[2,14,2304]{2,1,0:T(8,128)(2,1)S(1)}, u32[]{:S(2)}, u32[]{:S(2)}) %collective-permute-start) | collective-permute-done | bytes 129056 | tf_op jit(solution)/shard_map/ppermute | solution.py:24
  10.8 2.0 %shard_map.74 = (bf16[2304,256]{1,0:T(8,128)(2,1)S(1)}, bf16[2,256,2304]{2,1,0:T(8,128)(2,1)S(1)}, f32[2,256]{1,0:T(2,128)S(1)}) custom-call(bf16[1,2304,256]{2,1,0:T(8,128)(2,1)} %enc.1, bf16[1,3,256,2304]{3,2,1,0:T(8,128)(2,1)} %dec.1, f32[1,256]{1,0:T(1,128)} %bias.2, s32[1,1,16]{2,1,0:T(1,128)} %picks.1, ...), custom_call_target="tpu_custom_call" | custom-call | tf_op jit(solution)/shard_map/pallas_call | solution.py:36
  12.9 0.1 collective-permute-start.3
  13.0 2.2 %collective-permute-done.2.refs_2_ = bf16[2,14,2304]{2,1,0:T(8,128)(2,1)S(1)} collective-permute-done((bf16[2,14,2304]{2,1,0:T(8,128)(2,1)S(1)}, bf16[2,14,2304]{2,1,0:T(8,128)(2,1)S(1)}, u32[]{:S(2)}, u32[]{:S(2)}) %collective-permute-start.2) | collective-permute-done | bytes 129056 | tf_op jit(solution)/shard_map/ppermute | solution.py:24
  15.2 4.1 %collective-permute-done.1.refs_1_ = bf16[2,14,2304]{2,1,0:T(8,128)(2,1)S(1)} collective-permute-done((bf16[2,14,2304]{2,1,0:T(8,128)(2,1)S(1)}, bf16[2,14,2304]{2,1,0:T(8,128)(2,1)S(1)}, u32[]{:S(2)}, u32[]{:S(2)}) %collective-permute-start.1) | collective-permute-done | bytes 129056 | tf_op jit(solution)/shard_map/ppermute | solution.py:24
  19.3 0.0 collective-permute-done.3.refs_5_
  19.3 0.0 collective-permute-done.4.refs_7_
  19.3 0.5 %shard_map.75.feats = bf16[64,512]{1,0:T(8,128)(2,1)S(1)} custom-call(bf16[2,14,2304]{2,1,0:T(8,128)(2,1)S(1)} %collective-permute-done.after.refs_0_, bf16[2,14,2304]{2,1,0:T(8,128)(2,1)S(1)} %collective-permute-done.1.refs_1_, bf16[2,14,2304]{2,1,0:T(8,128)(2,1)S(1)} %collective-permute-done.2.refs_2_, bf16[2,14,2304]{2,1,0:T(8,128)(2,1)S(1)} %shard_map.73.refs_3_, ...), custom_call_target="tpu_custom_call" | custom-call | flops 301989888 | bytes 2359296 | tf_op jit(solution)/shard_map/pallas_call | solution.py:36
  19.8 1.6 %collective-permute-start.6 = (bf16[64,512]{1,0:T(8,128)(2,1)S(1)}, bf16[64,512]{1,0:T(8,128)(2,1)S(1)}, u32[]{:S(2)}, u32[]{:S(2)}) collective-permute-start(bf16[64,512]{1,0:T(8,128)(2,1)S(1)} %shard_map.75.feats), channel_id=1, source_target_pairs={{0,2},{2,0},{1,3},{3,1},{4,6},{6,4},{5,7},{7,5},{8,10},{10,8},{9,1... | collective-permute-start | bytes 196616 | tf_op jit(solution)/shard_map/ppermute | solution.py:24
  21.3 0.0 collective-permute-done.5.refs_1_.refs_2_
  21.3 0.0 copy-start
  21.3 0.5 %shard_map.76.base = f32[64,2304]{1,0:T(8,128)S(1)} custom-call(bf16[64,512]{1,0:T(8,128)(2,1)S(1)} %shard_map.75.feats, bf16[2,256,2304]{2,1,0:T(8,128)(2,1)S(1)} %get-tuple-element.14.refs_0_.refs_1_, bf16[3,256,2304]{2,1,0:T(8,128)(2,1)S(1)} %collective-permute-done.5.refs_1_.refs_2_), custom_call_target="tpu_custom_call" | custom-call | flops 150994944 | bytes 2359296 | tf_op jit(solution)/shard_map/pallas_call | solution.py:36
  21.9 2.2 %collective-permute-done.6.refs_0_ = bf16[64,512]{1,0:T(8,128)(2,1)S(1)} collective-permute-done((bf16[64,512]{1,0:T(8,128)(2,1)S(1)}, bf16[64,512]{1,0:T(8,128)(2,1)S(1)}, u32[]{:S(2)}, u32[]{:S(2)}) %collective-permute-start.6) | collective-permute-done | bytes 65568 | tf_op jit(solution)/shard_map/ppermute | solution.py:24
  24.1 0.0 copy-done
  24.1 0.1 shard_map.77
  24.2 0.1 collective-permute-start.7
  24.3 3.1 %collective-permute-start.8 = (bf16[14,2304]{1,0:T(8,128)(2,1)S(1)}, bf16[14,2304]{1,0:T(8,128)(2,1)S(1)}, u32[]{:S(2)}, u32[]{:S(2)}) collective-permute-start(bf16[14,2304]{1,0:T(8,128)(2,1)S(1)} %get-tuple-element.17), channel_id=1, source_target_pairs={{0,8},{4,12},{8,0},{12,4},{1,9},{5,13},{9,1},{13,5},{2,10},{6,14},... | collective-permute-start | bytes 193544 | tf_op jit(solution)/shard_map/ppermute | solution.py:24
  27.4 0.7 %collective-permute-start.9 = (bf16[14,2304]{1,0:T(8,128)(2,1)S(1)}, bf16[14,2304]{1,0:T(8,128)(2,1)S(1)}, u32[]{:S(2)}, u32[]{:S(2)}) collective-permute-start(bf16[14,2304]{1,0:T(8,128)(2,1)S(1)} %get-tuple-element.18), channel_id=1, source_target_pairs={{0,12},{4,0},{8,4},{12,8},{1,13},{5,1},{9,5},{13,9},{2,14},{6,2},{... | collective-permute-start | bytes 193544 | tf_op jit(solution)/shard_map/ppermute | solution.py:24
  28.1 2.4 %collective-permute-done.7.refs_0_ = bf16[14,2304]{1,0:T(8,128)(2,1)S(1)} collective-permute-done((bf16[14,2304]{1,0:T(8,128)(2,1)S(1)}, bf16[14,2304]{1,0:T(8,128)(2,1)S(1)}, u32[]{:S(2)}, u32[]{:S(2)}) %collective-permute-start.7) | collective-permute-done | bytes 64544 | tf_op jit(solution)/shard_map/ppermute | solution.py:24
  30.5 0.9 %collective-permute-done.8.refs_1_ = bf16[14,2304]{1,0:T(8,128)(2,1)S(1)} collective-permute-done((bf16[14,2304]{1,0:T(8,128)(2,1)S(1)}, bf16[14,2304]{1,0:T(8,128)(2,1)S(1)}, u32[]{:S(2)}, u32[]{:S(2)}) %collective-permute-start.8) | collective-permute-done | bytes 64544 | tf_op jit(solution)/shard_map/ppermute | solution.py:24
  31.4 0.4 %collective-permute-done.9.refs_2_ = bf16[14,2304]{1,0:T(8,128)(2,1)S(1)} collective-permute-done((bf16[14,2304]{1,0:T(8,128)(2,1)S(1)}, bf16[14,2304]{1,0:T(8,128)(2,1)S(1)}, u32[]{:S(2)}, u32[]{:S(2)}) %collective-permute-start.9) | collective-permute-done | bytes 64544 | tf_op jit(solution)/shard_map/ppermute | solution.py:24
  31.8 0.7 %shard_map.78 = bf16[1,14,2304]{2,1,0:T(8,128)(2,1)} custom-call(f32[14,2304]{1,0:T(8,128)S(1)} %get-tuple-element.15.own, bf16[14,2304]{1,0:T(8,128)(2,1)S(1)} %collective-permute-done.7.refs_0_, bf16[14,2304]{1,0:T(8,128)(2,1)S(1)} %collective-permute-done.8.refs_1_, bf16[14,2304]{1,0:T(8,128)(2,1)S(1)} %collective-permute-done.9.refs_2_), custom_call_target="tpu_custom_call" | custom-call | tf_op jit(solution)/shard_map/pallas_call | solution.py:36
Async XLA Ops:
  0.0 21.3 %collective-permute-start.5 = (bf16[3,256,2304]{2,1,0:T(8,128)(2,1)}, bf16[3,256,2304]{2,1,0:T(8,128)(2,1)S(1)}, u32[]{:S(2)}, u32[]{:S(2)}) collective-permute-start(bf16[3,256,2304]{2,1,0:T(8,128)(2,1)} %bitcast.2), channel_id=1, source_target_pairs={{0,1},{1,0},{2,3},{3,2},{4,5},{5,4},{6,7},{7,6},{8,9},{9,8},{10,11... | collective-permute-start | bytes 10616840 | tf_op jit(solution)/shard_map/ppermute | solution.py:24
  0.5 18.8 %collective-permute-start.4 = (bf16[2304,256]{1,0:T(8,128)(2,1)}, bf16[2304,256]{1,0:T(8,128)(2,1)S(1)}, u32[]{:S(2)}, u32[]{:S(2)}) collective-permute-start(bf16[2304,256]{1,0:T(8,128)(2,1)} %bitcast.3), channel_id=1, source_target_pairs={{0,1},{1,0},{2,3},{3,2},{4,5},{5,4},{6,7},{7,6},{8,9},{9,8},{10,11... | collective-permute-start | bytes 3538952 | tf_op jit(solution)/shard_map/ppermute | solution.py:24
  1.5 9.4 %collective-permute-start = (bf16[2,14,2304]{2,1,0:T(8,128)(2,1)S(1)}, bf16[2,14,2304]{2,1,0:T(8,128)(2,1)S(1)}, u32[]{:S(2)}, u32[]{:S(2)}) collective-permute-start(bf16[2,14,2304]{2,1,0:T(8,128)(2,1)S(1)} %shard_map.73.refs_3_), channel_id=1, source_target_pairs={{0,12},{4,0},{8,4},{12,8},{1,13},{5,1},{9,5},{13,9},{2,14},{6,2},{... | collective-permute-start | bytes 387080 | tf_op jit(solution)/shard_map/ppermute | solution.py:24
  6.6 8.6 %collective-permute-start.2 = (bf16[2,14,2304]{2,1,0:T(8,128)(2,1)S(1)}, bf16[2,14,2304]{2,1,0:T(8,128)(2,1)S(1)}, u32[]{:S(2)}, u32[]{:S(2)}) collective-permute-start(bf16[2,14,2304]{2,1,0:T(8,128)(2,1)S(1)} %shard_map.73.refs_3_), channel_id=1, source_target_pairs={{0,4},{4,8},{8,12},{12,0},{1,5},{5,9},{9,13},{13,1},{2,6},{6,10},{... | collective-permute-start | bytes 387080 | tf_op jit(solution)/shard_map/ppermute | solution.py:24
  6.6 12.7 %collective-permute-start.1 = (bf16[2,14,2304]{2,1,0:T(8,128)(2,1)S(1)}, bf16[2,14,2304]{2,1,0:T(8,128)(2,1)S(1)}, u32[]{:S(2)}, u32[]{:S(2)}) collective-permute-start(bf16[2,14,2304]{2,1,0:T(8,128)(2,1)S(1)} %shard_map.73.refs_3_), channel_id=1, source_target_pairs={{0,8},{4,12},{8,0},{12,4},{1,9},{5,13},{9,1},{13,5},{2,10},{6,14},... | collective-permute-start | bytes 387080 | tf_op jit(solution)/shard_map/ppermute | solution.py:24
  12.9 6.4 %collective-permute-start.3 = (f32[2,256]{1,0:T(2,128)S(1)}, f32[2,256]{1,0:T(2,128)S(1)}, u32[]{:S(2)}, u32[]{:S(2)}) collective-permute-start(f32[2,256]{1,0:T(2,128)S(1)} %get-tuple-element.12.refs_4_), channel_id=1, source_target_pairs={{0,1},{1,0},{2,3},{3,2},{4,5},{5,4},{6,7},{7,6},{8,9},{9,8},{10,11... | collective-permute-start | bytes 6152 | tf_op jit(solution)/shard_map/ppermute | solution.py:24
  19.8 4.3 %collective-permute-start.6 = (bf16[64,512]{1,0:T(8,128)(2,1)S(1)}, bf16[64,512]{1,0:T(8,128)(2,1)S(1)}, u32[]{:S(2)}, u32[]{:S(2)}) collective-permute-start(bf16[64,512]{1,0:T(8,128)(2,1)S(1)} %shard_map.75.feats), channel_id=1, source_target_pairs={{0,2},{2,0},{1,3},{3,1},{4,6},{6,4},{5,7},{7,5},{8,10},{10,8},{9,1... | collective-permute-start | bytes 196616 | tf_op jit(solution)/shard_map/ppermute | solution.py:24
  21.3 2.8 %copy-start = (f32[1,2304]{1,0:T(1,128)S(1)}, f32[1,2304]{1,0:T(1,128)}, u32[]{:S(2)}) copy-start(f32[1,2304]{1,0:T(1,128)} %bias.3) | copy-start | bytes 27652
  24.2 6.3 %collective-permute-start.7 = (bf16[14,2304]{1,0:T(8,128)(2,1)S(1)}, bf16[14,2304]{1,0:T(8,128)(2,1)S(1)}, u32[]{:S(2)}, u32[]{:S(2)}) collective-permute-start(bf16[14,2304]{1,0:T(8,128)(2,1)S(1)} %get-tuple-element.16), channel_id=1, source_target_pairs={{0,4},{4,8},{8,12},{12,0},{1,5},{5,9},{9,13},{13,1},{2,6},{6,10},{... | collective-permute-start | bytes 193544 | tf_op jit(solution)/shard_map/ppermute | solution.py:24
  24.3 7.2 %collective-permute-start.8 = (bf16[14,2304]{1,0:T(8,128)(2,1)S(1)}, bf16[14,2304]{1,0:T(8,128)(2,1)S(1)}, u32[]{:S(2)}, u32[]{:S(2)}) collective-permute-start(bf16[14,2304]{1,0:T(8,128)(2,1)S(1)} %get-tuple-element.17), channel_id=1, source_target_pairs={{0,8},{4,12},{8,0},{12,4},{1,9},{5,13},{9,1},{13,5},{2,10},{6,14},... | collective-permute-start | bytes 193544 | tf_op jit(solution)/shard_map/ppermute | solution.py:24
  27.4 4.4 %collective-permute-start.9 = (bf16[14,2304]{1,0:T(8,128)(2,1)S(1)}, bf16[14,2304]{1,0:T(8,128)(2,1)S(1)}, u32[]{:S(2)}, u32[]{:S(2)}) collective-permute-start(bf16[14,2304]{1,0:T(8,128)(2,1)S(1)} %get-tuple-element.18), channel_id=1, source_target_pairs={{0,12},{4,0},{8,4},{12,8},{1,13},{5,1},{9,5},{13,9},{2,14},{6,2},{... | collective-permute-start | bytes 193544 | tf_op jit(solution)/shard_map/ppermute | solution.py:24

commit v4 on v3

--- a/solution.py
+++ b/solution.py
@@ -22,6 +22,11 @@
 def rotated(value, axis, by):
     count = lax.axis_size(axis)
     return lax.ppermute(value, axis, [(i, (i + by) % count) for i in range(count)])
+
+
+def paired(value, axis, by):
+    count = lax.axis_size(axis)
+    return lax.ppermute(value, axis, [(i, i ^ by) for i in range(count)])
 
 
 def near(value):
@@ -79,53 +84,56 @@
         c.wait()
 
 
-def encode_body(chips, cores, *refs):
-    got, smalls, encs = refs[:chips][::-1], refs[chips : chips + cores], refs[chips + cores : chips + 2 * cores]
-    out, x = refs[chips + 2 * cores :]
+def encode_body(count, cores, earlier, *refs):
+    refs = refs[earlier:]
+    got, refs = refs[:count], refs[count:]
+    smalls, encs, (out, x) = refs[:cores], refs[cores : 2 * cores], refs[2 * cores :]
     rows = got[0].shape[1]
-    half = chips * SLOT
-    for k in range(chips):
+    half = count * SLOT
+    for i in range(count):
         for c in range(2):
-            x[c * half + k * SLOT : c * half + k * SLOT + rows, :] = got[k][c]
+            x[c * half + i * SLOT : c * half + i * SLOT + rows, :] = got[i][c]
     width = encs[0].shape[1]
     for j in range(cores):
         h = jnp.dot(x[...], encs[j][...], preferred_element_type=jnp.float32)
         pre = jnp.where(smalls[j][1:2, :] > 0.5, h[half:], h[:half]) + smalls[j][0:1, :]
-        out[:, j * width : (j + 1) * width] = jnp.maximum(pre, 0.0).astype(jnp.bfloat16)
-
-
-def dots(feats, decs, level, cores):
+        feats = jnp.maximum(pre, 0.0).astype(jnp.bfloat16)
+        for i in range(count):
+            out[i, :, j * width : (j + 1) * width] = feats[i * SLOT : i * SLOT + rows]
+
+
+def dots(feats, decs, level, x):
     width = decs[0].shape[1]
+    count, rows = feats.shape[:2]
+    for i in range(count):
+        x[i * SLOT : i * SLOT + rows, :] = feats[i]
     total = None
-    for j in range(cores):
+    for j, dec in enumerate(decs):
         one = jnp.dot(
-            feats[:, j * width : (j + 1) * width],
-            decs[j][level],
-            preferred_element_type=jnp.float32,
+            x[:, j * width : (j + 1) * width], dec[level], preferred_element_type=jnp.float32
         )
         total = one if total is None else total + one
     return total
 
 
 def own_body(cores, feats, *refs):
-    decs, out = refs[:cores], refs[cores]
-    out[...] = dots(feats, decs, 0, cores)
-
-
-def rest_body(chips, cores, depth, rows, base, bias, *refs):
+    decs, (out, x) = refs[:cores], refs[-2:]
+    out[...] = dots(feats, decs, 0, x)
+
+
+def rest_body(cores, depth, slots, rows, base, bias, *refs):
     known, decs = refs[:depth], refs[depth : depth + cores]
-    outs = refs[depth + cores :]
-    outs, total = outs[:-1], outs[-1]
+    outs, (total, x) = refs[depth + cores : -2], refs[-2:]
     total[...] = base[...]
     for k in range(depth):
 
         @pl.when(lax.axis_index("layer") > k)
         def _():
-            total[...] += dots(known[k], decs, k + 1, cores)
-
-    outs[0][...] = total[:rows] + bias[...]
-    for k in range(1, chips):
-        outs[k][...] = total[k * SLOT : k * SLOT + rows].astype(jnp.bfloat16)
+            total[...] += dots(known[k], decs, k + 1, x)
+
+    for i, slot in enumerate(slots):
+        part = total[i * SLOT : i * SLOT + rows]
+        outs[i][...] = part + bias[...] if slot == 0 else part.astype(jnp.bfloat16)
 
 
 def sum_body(own, *refs):
@@ -151,7 +159,8 @@
         [far(v) for v in (clean_resid, corrupt_resid)],
         (dma((2,)),),
     )
-    got = [rotated(both, "feat", k) for k in range(1, chips)]
+    relayed = [k for k in range(2, chips) if k % 2]
+    got = [both] + [None if k in relayed else paired(both, "feat", k) for k in range(1, chips)]
     enc, dec, small = call(
         functools.partial(load_body, depth + 1),
         (
@@ -160,45 +169,61 @@
             VMEM((2, width), f32),
         ),
         (hbm,) * 4 + (any_,),
-        [far(v) for v in (enc_weight, dec_weight, enc_bias, patch_index)] + [got[2]],
+        [far(v) for v in (enc_weight, dec_weight, enc_bias, patch_index)] + [got[1]],
         (
             VMEM((1, width), f32),
             pltpu.SMEM(patch_index.shape[1:], jnp.int32),
             dma((depth + 4,)),
         ),
     )
+    if relayed:
+        *held, small = lax.optimization_barrier((*[got[k - 1] for k in relayed], small))
+        for k, v in zip(relayed, held):
+            got[k - 1] = v
+            got[k] = paired(v, "feat", 1)
     smalls = [small] + [rotated(small, "dec", j) for j in range(1, cores)]
-    got = [both] + got
     encs = [enc] + [rotated(enc_weight[0], "dec", j) for j in range(1, cores)]
     decs = [dec] + [rotated(dec_weight[0], "dec", j) for j in range(1, cores)]
-    feats = call(
-        functools.partial(encode_body, chips, cores),
-        VMEM((chips * SLOT, cores * width), bf16),
-        (VMEM,) * (chips + 2 * cores),
-        [near(v) for v in (*got[::-1], *smalls, *encs)],
-        (VMEM((2 * chips * SLOT, model), bf16),),
-        flops=4 * chips * SLOT * model * width * cores,
-        moved=cores * width * model * 2,
-    )
-    known = [rotated(feats, "layer", o) for o in range(1, depth + 1)]
-    base = call(
-        functools.partial(own_body, cores),
-        VMEM((chips * SLOT, model), f32),
-        (VMEM,) * (1 + cores),
-        [near(v) for v in (feats, *decs)],
-        flops=2 * chips * SLOT * model * width * cores,
-        moved=cores * width * model * 2,
-    )
-    parts = call(
-        functools.partial(rest_body, chips, cores, depth, rows),
-        (VMEM((rows, model), f32),) + (VMEM((rows, model), bf16),) * (chips - 1),
-        (VMEM,) * (2 + depth + cores),
-        [near(v) for v in (base, dec_bias, *known, *decs)],
-        (VMEM((chips * SLOT, model), f32),),
-        flops=2 * chips * SLOT * model * width * cores * depth,
-        moved=cores * width * model * 2 * depth,
-    )
-    back = [rotated(parts[k], "feat", -k) for k in range(chips - 1, 0, -1)]
+    wide = cores * width
+    parts = [None] * chips
+    before_encode = before_own = ()
+    direct = [k for k in range(chips) if k not in relayed]
+    for slots in filter(None, (direct, relayed)):
+        n = len(slots)
+        feats = call(
+            functools.partial(encode_body, n, cores, len(before_encode)),
+            VMEM((n, rows, wide), bf16),
+            (any_,) * len(before_encode) + (VMEM,) * (n + 2 * cores),
+            [near(v) for v in (*before_encode, *[got[k] for k in slots], *smalls, *encs)],
+            (VMEM((2 * n * SLOT, model), bf16),),
+            flops=4 * n * SLOT * model * wide,
+            moved=wide * model * 2,
+        )
+        known = [rotated(feats, "layer", o) for o in range(1, depth + 1)]
+        base = call(
+            functools.partial(own_body, cores),
+            VMEM((n * SLOT, model), f32),
+            (VMEM,) * (1 + cores) + (any_,) * len(before_own),
+            [near(v) for v in (feats, *decs, *before_own)],
+            (VMEM((n * SLOT, wide), bf16),),
+            flops=2 * n * SLOT * model * wide,
+            moved=wide * model * 2,
+        )
+        outs = call(
+            functools.partial(rest_body, cores, depth, slots, rows),
+            tuple(VMEM((rows, model), bf16 if k else f32) for k in slots),
+            (VMEM,) * (2 + depth + cores),
+            [near(v) for v in (base, dec_bias, *known, *decs)],
+            (VMEM((n * SLOT, model), f32), VMEM((n * SLOT, wide), bf16)),
+            flops=2 * n * SLOT * model * wide * depth,
+            moved=wide * model * 2 * depth,
+        )
+        for k, out in zip(slots, outs):
+            parts[k] = out
+        before_encode, before_own = (base,), (outs[-1],)
+    if relayed:
+        parts[1], parts[-1] = lax.optimization_barrier((parts[1], parts[-1]))
+    back = [paired(parts[k], "feat", k) for k in range(chips - 1, 0, -1)]
     return call(
         sum_body,
         jax.ShapeDtypeStruct((1, rows, model), bf16),

time: 32.6 us -> 31.5 us (0.966)
  waiting for transfers between devices: 15.5 us -> 11.6 us
  starting transfers between devices: 12.1 us -> 14 us
  Pallas kernels: 4.77 us -> 5.72 us
    ppermute x10 -> x5, waiting for transfers between devices: 15.5 us -> 1.19 us  [rotated(): lax.ppermute(value, axis, [(i, (i + by) % count) for i in range(count)])]
    ppermute x0 -> x6, starting transfers between devices: none -> 10.4 us  [paired(): return lax.ppermute(value, axis, [(i, i ^ by) for i in range(count)])]
    ppermute x0 -> x6, waiting for transfers between devices: none -> 10.4 us  [paired(): return lax.ppermute(value, axis, [(i, i ^ by) for i in range(count)])]
    ppermute x10 -> x5, starting transfers between devices: 12.1 us -> 3.63 us  [rotated(): lax.ppermute(value, axis, [(i, (i + by) % count) for i in range(count)])]
    pallas_call x6 -> x9, Pallas kernels: 4.77 us -> 5.72 us  [call(): pl.pallas_call(body, out_shape=outs, in_specs=[pl.BlockSpec(memory_space=...]
  transfers between devices with their start and end apart: 10 -> 11, of which waited for: 7 -> 7; matrix products, arithmetic and copies ran while one was open for 0% -> 0% of each run, Pallas kernels for 12% -> 16%
where the time goes in v4:
time: 31.5 us; the launch traced here: 31.4 us
  starting transfers between devices  14 us (44%)
  waiting for transfers between devices  11.6 us (37%)
  Pallas kernels  5.72 us (18%)
    ppermute x6, starting transfers between devices, paired(): return lax.ppermute(value, axis, [(i, i ^ by) for i in range(count)])  10.4 us
    ppermute x6, waiting for transfers between devices, paired(): return lax.ppermute(value, axis, [(i, i ^ by) for i in range(count)])  10.4 us
    pallas_call x9, Pallas kernels, call(): pl.pallas_call(body, out_shape=outs, in_specs=[pl.BlockSpec(memory_space=...  5.72 us
    ppermute x5, starting transfers between devices, rotated(): lax.ppermute(value, axis, [(i, (i + by) % count) for i in range(count)])  3.63 us
    ppermute x5, waiting for transfers between devices, rotated(): lax.ppermute(value, axis, [(i, (i + by) % count) for i in range(count)])  1.19 us
  transfers between devices with their start and end apart: 11, of which 7 were waited for; matrix products, arithmetic and copies ran while one was open for 0% of the time, Pallas kernels for 16%

profile of v4, /device:TPU:0, one launch (start us, length us, event | category | flops | bytes accessed | tf_op | source)
XLA Modules:
  0.0 31.4 jit_solution(7807975392178151778)
XLA Ops:
  0.0 0.5 %collective-permute-start.4 = (bf16[3,256,2304]{2,1,0:T(8,128)(2,1)}, bf16[3,256,2304]{2,1,0:T(8,128)(2,1)S(1)}, u32[]{:S(2)}, u32[]{:S(2)}) collective-permute-start(bf16[3,256,2304]{2,1,0:T(8,128)(2,1)} %bitcast.2), channel_id=1, source_target_pairs={{0,1},{1,0},{2,3},{3,2},{4,5},{5,4},{6,7},{7,6},{8,9},{9,8},{10,11... | collective-permute-start | bytes 10616840 | tf_op jit(solution)/shard_map/ppermute | solution.py:24
  0.5 0.1 collective-permute-start.3
  0.5 0.9 %shard_map.73.refs_0_ = bf16[2,14,2304]{2,1,0:T(8,128)(2,1)S(1)} custom-call(bf16[1,14,2304]{2,1,0:T(8,128)(2,1)} %clean.1, bf16[1,14,2304]{2,1,0:T(8,128)(2,1)} %corrupt.1), custom_call_target="tpu_custom_call" | custom-call | tf_op jit(solution)/shard_map/pallas_call | solution.py:41
  1.5 3.1 %collective-permute-start = (bf16[2,14,2304]{2,1,0:T(8,128)(2,1)S(1)}, bf16[2,14,2304]{2,1,0:T(8,128)(2,1)S(1)}, u32[]{:S(2)}, u32[]{:S(2)}) collective-permute-start(bf16[2,14,2304]{2,1,0:T(8,128)(2,1)S(1)} %shard_map.73.refs_0_), channel_id=1, source_target_pairs={{0,4},{4,0},{8,12},{12,8},{1,5},{5,1},{9,13},{13,9},{2,6},{6,2},{1... | collective-permute-start | bytes 387080 | tf_op jit(solution)/shard_map/ppermute | solution.py:29
  4.5 2.6 %collective-permute-start.1 = (bf16[2,14,2304]{2,1,0:T(8,128)(2,1)S(1)}, bf16[2,14,2304]{2,1,0:T(8,128)(2,1)S(1)}, u32[]{:S(2)}, u32[]{:S(2)}) collective-permute-start(bf16[2,14,2304]{2,1,0:T(8,128)(2,1)S(1)} %shard_map.73.refs_0_), channel_id=1, source_target_pairs={{0,8},{4,12},{8,0},{12,4},{1,9},{5,13},{9,1},{13,5},{2,10},{6,14},... | collective-permute-start | bytes 387080 | tf_op jit(solution)/shard_map/ppermute | solution.py:29
  7.1 4.2 %collective-permute-done.after.refs_1_ = bf16[2,14,2304]{2,1,0:T(8,128)(2,1)S(1)} collective-permute-done((bf16[2,14,2304]{2,1,0:T(8,128)(2,1)S(1)}, bf16[2,14,2304]{2,1,0:T(8,128)(2,1)S(1)}, u32[]{:S(2)}, u32[]{:S(2)}) %collective-permute-start) | collective-permute-done | bytes 129056 | tf_op jit(solution)/shard_map/ppermute | solution.py:29
  11.3 2.0 %shard_map.74 = (bf16[2304,256]{1,0:T(8,128)(2,1)S(1)}, bf16[2,256,2304]{2,1,0:T(8,128)(2,1)S(1)}, f32[2,256]{1,0:T(2,128)S(1)}) custom-call(bf16[1,2304,256]{2,1,0:T(8,128)(2,1)} %enc.1, bf16[1,3,256,2304]{3,2,1,0:T(8,128)(2,1)} %dec.1, f32[1,256]{1,0:T(1,128)} %bias.3, s32[1,1,16]{2,1,0:T(1,128)} %picks.1, ...), custom_call_target="tpu_custom_call" | custom-call | tf_op jit(solution)/shard_map/pallas_call | solution.py:41
  13.3 0.8 %collective-permute-done.1.refs_2_ = bf16[2,14,2304]{2,1,0:T(8,128)(2,1)S(1)} collective-permute-done((bf16[2,14,2304]{2,1,0:T(8,128)(2,1)S(1)}, bf16[2,14,2304]{2,1,0:T(8,128)(2,1)S(1)}, u32[]{:S(2)}, u32[]{:S(2)}) %collective-permute-start.1) | collective-permute-done | bytes 129056 | tf_op jit(solution)/shard_map/ppermute | solution.py:29
  14.1 0.4 %collective-permute-start.6 = (bf16[2,14,2304]{2,1,0:T(8,128)(2,1)S(1)}, bf16[2,14,2304]{2,1,0:T(8,128)(2,1)S(1)}, u32[]{:S(2)}, u32[]{:S(2)}) collective-permute-start(bf16[2,14,2304]{2,1,0:T(8,128)(2,1)S(1)} %collective-permute-done.1.refs_2_), channel_id=1, source_target_pairs={{0,4},{4,0},{8,12},{12,8},{1,5},{5,1},{9,13},{13,9},{2,6},{6,2},{1... | collective-permute-start | bytes 387080 | tf_op jit(solution)/shard_map/ppermute | solution.py:29
  14.6 0.0 collective-permute-start.2
  14.6 1.2 %collective-permute-done.2.refs_4_.refs_3_ = f32[2,256]{1,0:T(2,128)S(1)} collective-permute-done((f32[2,256]{1,0:T(2,128)S(1)}, f32[2,256]{1,0:T(2,128)S(1)}, u32[]{:S(2)}, u32[]{:S(2)}) %collective-permute-start.2) | collective-permute-done | bytes 2080 | tf_op jit(solution)/shard_map/ppermute | solution.py:24
  15.7 0.0 collective-permute-done.3.refs_6_.refs_5_
  15.7 0.5 %shard_map.75.feats = bf16[3,14,512]{2,1,0:T(8,128)(2,1)S(1)} custom-call(bf16[2,14,2304]{2,1,0:T(8,128)(2,1)S(1)} %shard_map.73.refs_0_, bf16[2,14,2304]{2,1,0:T(8,128)(2,1)S(1)} %collective-permute-done.after.refs_1_, bf16[2,14,2304]{2,1,0:T(8,128)(2,1)S(1)} %collective-permute-done.1.refs_2_, f32[2,256]{1,0:T(2,128)S(1)} %get-tuple-element.17.refs_3_.refs_2_, ...), custom_call_target="tpu_custom_call" | custom-call | flops 226492416 | bytes 2359296 | tf_op jit(solution)/shard_map/pallas_call | solution.py:41
  16.3 1.6 %collective-permute-start.5 = (bf16[3,14,512]{2,1,0:T(8,128)(2,1)S(1)}, bf16[3,14,512]{2,1,0:T(8,128)(2,1)S(1)}, u32[]{:S(2)}, u32[]{:S(2)}) collective-permute-start(bf16[3,14,512]{2,1,0:T(8,128)(2,1)S(1)} %shard_map.75.feats), channel_id=1, source_target_pairs={{0,2},{2,0},{1,3},{3,1},{4,6},{6,4},{5,7},{7,5},{8,10},{10,8},{9,1... | collective-permute-start | bytes 129032 | tf_op jit(solution)/shard_map/ppermute | solution.py:24
  17.8 0.0 collective-permute-done.4.refs_1_.refs_2_
  17.8 0.5 %shard_map.76.base.refs_0_ = f32[48,2304]{1,0:T(8,128)S(1)} custom-call(bf16[3,14,512]{2,1,0:T(8,128)(2,1)S(1)} %shard_map.75.feats, bf16[2,256,2304]{2,1,0:T(8,128)(2,1)S(1)} %get-tuple-element.19.refs_0_.refs_1_, bf16[3,256,2304]{2,1,0:T(8,128)(2,1)S(1)} %collective-permute-done.4.refs_1_.refs_2_), custom_call_target="tpu_custom_call" | custom-call | flops 113246208 | bytes 2359296 | tf_op jit(solution)/shard_map/pallas_call | solution.py:41
  18.4 0.0 copy-start
  18.4 0.9 %collective-permute-done.6.refs_1_ = bf16[2,14,2304]{2,1,0:T(8,128)(2,1)S(1)} collective-permute-done((bf16[2,14,2304]{2,1,0:T(8,128)(2,1)S(1)}, bf16[2,14,2304]{2,1,0:T(8,128)(2,1)S(1)}, u32[]{:S(2)}, u32[]{:S(2)}) %collective-permute-start.6) | collective-permute-done | bytes 129056 | tf_op jit(solution)/shard_map/ppermute | solution.py:29
  19.3 0.5 %shard_map.78.feats = bf16[1,14,512]{2,1,0:T(8,128)(2,1)S(1)} custom-call(f32[48,2304]{1,0:T(8,128)S(1)} %shard_map.76.base.refs_0_, bf16[2,14,2304]{2,1,0:T(8,128)(2,1)S(1)} %collective-permute-done.6.refs_1_, f32[2,256]{1,0:T(2,128)S(1)} %get-tuple-element.17.refs_3_.refs_2_, f32[2,256]{1,0:T(2,128)S(1)} %collective-permute-done.2.refs_4_.refs_3_, ...), custom_call_target="tpu_custom_call" | custom-call | flops 75497472 | bytes 2359296 | tf_op jit(solution)/shard_map/pallas_call | solution.py:41
  19.8 1.6 %collective-permute-start.7 = (bf16[1,14,512]{2,1,0:T(8,128)(2,1)S(1)}, bf16[1,14,512]{2,1,0:T(8,128)(2,1)S(1)}, u32[]{:S(2)}, u32[]{:S(2)}) collective-permute-start(bf16[1,14,512]{2,1,0:T(8,128)(2,1)S(1)} %shard_map.78.feats), channel_id=1, source_target_pairs={{0,2},{2,0},{1,3},{3,1},{4,6},{6,4},{5,7},{7,5},{8,10},{10,8},{9,1... | collective-permute-start | bytes 43016 | tf_op jit(solution)/shard_map/ppermute | solution.py:24
  21.4 0.0 collective-permute-done.5.refs_0_
  21.4 0.0 copy-done
  21.4 0.1 shard_map.77
  21.4 1.7 %collective-permute-start.9 = (bf16[14,2304]{1,0:T(8,128)(2,1)S(1)}, bf16[14,2304]{1,0:T(8,128)(2,1)S(1)}, u32[]{:S(2)}, u32[]{:S(2)}) collective-permute-start(bf16[14,2304]{1,0:T(8,128)(2,1)S(1)} %get-tuple-element.22.refs_2_), channel_id=1, source_target_pairs={{0,8},{4,12},{8,0},{12,4},{1,9},{5,13},{9,1},{13,5},{2,10},{6,14},... | collective-permute-start | bytes 193544 | tf_op jit(solution)/shard_map/ppermute | solution.py:29
  23.2 0.4 %shard_map.79.base = f32[16,2304]{1,0:T(8,128)S(1)} custom-call(bf16[1,14,512]{2,1,0:T(8,128)(2,1)S(1)} %shard_map.78.feats, bf16[2,256,2304]{2,1,0:T(8,128)(2,1)S(1)} %get-tuple-element.19.refs_0_.refs_1_, bf16[3,256,2304]{2,1,0:T(8,128)(2,1)S(1)} %collective-permute-done.4.refs_1_.refs_2_, bf16[14,2304]{1,0:T(8,128)(2,1)S(1)} %get-tuple-element.22.refs_2_), custom_call_target="tpu_custom_call" | custom-call | flops 37748736 | bytes 2359296 | tf_op jit(solution)/shard_map/pallas_call | solution.py:41
  23.6 0.0 collective-permute-done.7.refs_0_
  23.6 2.5 %collective-permute-start.8 = (bf16[14,2304]{1,0:T(8,128)(2,1)S(1)}, bf16[14,2304]{1,0:T(8,128)(2,1)S(1)}, u32[]{:S(2)}, u32[]{:S(2)}) collective-permute-start(bf16[14,2304]{1,0:T(8,128)(2,1)S(1)} %shard_map.80), channel_id=1, source_target_pairs={{0,12},{4,8},{8,4},{12,0},{1,13},{5,9},{9,5},{13,1},{2,14},{6,10},... | collective-permute-start | bytes 193544 | tf_op jit(solution)/shard_map/ppermute | solution.py:29
  26.2 0.0 collective-permute-start.10
  26.2 2.2 %collective-permute-done.9.refs_1_ = bf16[14,2304]{1,0:T(8,128)(2,1)S(1)} collective-permute-done((bf16[14,2304]{1,0:T(8,128)(2,1)S(1)}, bf16[14,2304]{1,0:T(8,128)(2,1)S(1)}, u32[]{:S(2)}, u32[]{:S(2)}) %collective-permute-start.9) | collective-permute-done | bytes 64544 | tf_op jit(solution)/shard_map/ppermute | solution.py:29
  28.3 1.6 %collective-permute-done.8.refs_0_ = bf16[14,2304]{1,0:T(8,128)(2,1)S(1)} collective-permute-done((bf16[14,2304]{1,0:T(8,128)(2,1)S(1)}, bf16[14,2304]{1,0:T(8,128)(2,1)S(1)}, u32[]{:S(2)}, u32[]{:S(2)}) %collective-permute-start.8) | collective-permute-done | bytes 64544 | tf_op jit(solution)/shard_map/ppermute | solution.py:29
  29.9 0.8 %collective-permute-done.10.refs_2_ = bf16[14,2304]{1,0:T(8,128)(2,1)S(1)} collective-permute-done((bf16[14,2304]{1,0:T(8,128)(2,1)S(1)}, bf16[14,2304]{1,0:T(8,128)(2,1)S(1)}, u32[]{:S(2)}, u32[]{:S(2)}) %collective-permute-start.10) | collective-permute-done | bytes 64544 | tf_op jit(solution)/shard_map/ppermute | solution.py:29
  30.7 0.7 %shard_map.81 = bf16[1,14,2304]{2,1,0:T(8,128)(2,1)} custom-call(f32[14,2304]{1,0:T(8,128)S(1)} %get-tuple-element.20.own, bf16[14,2304]{1,0:T(8,128)(2,1)S(1)} %collective-permute-done.8.refs_0_, bf16[14,2304]{1,0:T(8,128)(2,1)S(1)} %collective-permute-done.9.refs_1_, bf16[14,2304]{1,0:T(8,128)(2,1)S(1)} %collective-permute-done.10.refs_2_), custom_call_target="tpu_custom_call" | custom-call | tf_op jit(solution)/shard_map/pallas_call | solution.py:41
  (1 shorter events, 0.0 us)
Async XLA Ops:
  0.0 17.8 %collective-permute-start.4 = (bf16[3,256,2304]{2,1,0:T(8,128)(2,1)}, bf16[3,256,2304]{2,1,0:T(8,128)(2,1)S(1)}, u32[]{:S(2)}, u32[]{:S(2)}) collective-permute-start(bf16[3,256,2304]{2,1,0:T(8,128)(2,1)} %bitcast.2), channel_id=1, source_target_pairs={{0,1},{1,0},{2,3},{3,2},{4,5},{5,4},{6,7},{7,6},{8,9},{9,8},{10,11... | collective-permute-start | bytes 10616840 | tf_op jit(solution)/shard_map/ppermute | solution.py:24
  0.5 15.3 %collective-permute-start.3 = (bf16[2304,256]{1,0:T(8,128)(2,1)}, bf16[2304,256]{1,0:T(8,128)(2,1)S(1)}, u32[]{:S(2)}, u32[]{:S(2)}) collective-permute-start(bf16[2304,256]{1,0:T(8,128)(2,1)} %bitcast.3), channel_id=1, source_target_pairs={{0,1},{1,0},{2,3},{3,2},{4,5},{5,4},{6,7},{7,6},{8,9},{9,8},{10,11... | collective-permute-start | bytes 3538952 | tf_op jit(solution)/shard_map/ppermute | solution.py:24
  1.5 9.8 %collective-permute-start = (bf16[2,14,2304]{2,1,0:T(8,128)(2,1)S(1)}, bf16[2,14,2304]{2,1,0:T(8,128)(2,1)S(1)}, u32[]{:S(2)}, u32[]{:S(2)}) collective-permute-start(bf16[2,14,2304]{2,1,0:T(8,128)(2,1)S(1)} %shard_map.73.refs_0_), channel_id=1, source_target_pairs={{0,4},{4,0},{8,12},{12,8},{1,5},{5,1},{9,13},{13,9},{2,6},{6,2},{1... | collective-permute-start | bytes 387080 | tf_op jit(solution)/shard_map/ppermute | solution.py:29
  4.5 9.6 %collective-permute-start.1 = (bf16[2,14,2304]{2,1,0:T(8,128)(2,1)S(1)}, bf16[2,14,2304]{2,1,0:T(8,128)(2,1)S(1)}, u32[]{:S(2)}, u32[]{:S(2)}) collective-permute-start(bf16[2,14,2304]{2,1,0:T(8,128)(2,1)S(1)} %shard_map.73.refs_0_), channel_id=1, source_target_pairs={{0,8},{4,12},{8,0},{12,4},{1,9},{5,13},{9,1},{13,5},{2,10},{6,14},... | collective-permute-start | bytes 387080 | tf_op jit(solution)/shard_map/ppermute | solution.py:29
  14.1 5.1 %collective-permute-start.6 = (bf16[2,14,2304]{2,1,0:T(8,128)(2,1)S(1)}, bf16[2,14,2304]{2,1,0:T(8,128)(2,1)S(1)}, u32[]{:S(2)}, u32[]{:S(2)}) collective-permute-start(bf16[2,14,2304]{2,1,0:T(8,128)(2,1)S(1)} %collective-permute-done.1.refs_2_), channel_id=1, source_target_pairs={{0,4},{4,0},{8,12},{12,8},{1,5},{5,1},{9,13},{13,9},{2,6},{6,2},{1... | collective-permute-start | bytes 387080 | tf_op jit(solution)/shard_map/ppermute | solution.py:29
  14.6 1.2 %collective-permute-start.2 = (f32[2,256]{1,0:T(2,128)S(1)}, f32[2,256]{1,0:T(2,128)S(1)}, u32[]{:S(2)}, u32[]{:S(2)}) collective-permute-start(f32[2,256]{1,0:T(2,128)S(1)} %get-tuple-element.17.refs_3_.refs_2_), channel_id=1, source_target_pairs={{0,1},{1,0},{2,3},{3,2},{4,5},{5,4},{6,7},{7,6},{8,9},{9,8},{10,11... | collective-permute-start | bytes 6152 | tf_op jit(solution)/shard_map/ppermute | solution.py:24
  16.3 5.1 %collective-permute-start.5 = (bf16[3,14,512]{2,1,0:T(8,128)(2,1)S(1)}, bf16[3,14,512]{2,1,0:T(8,128)(2,1)S(1)}, u32[]{:S(2)}, u32[]{:S(2)}) collective-permute-start(bf16[3,14,512]{2,1,0:T(8,128)(2,1)S(1)} %shard_map.75.feats), channel_id=1, source_target_pairs={{0,2},{2,0},{1,3},{3,1},{4,6},{6,4},{5,7},{7,5},{8,10},{10,8},{9,1... | collective-permute-start | bytes 129032 | tf_op jit(solution)/shard_map/ppermute | solution.py:24
  18.4 3.0 %copy-start = (f32[1,2304]{1,0:T(1,128)S(1)}, f32[1,2304]{1,0:T(1,128)}, u32[]{:S(2)}) copy-start(f32[1,2304]{1,0:T(1,128)} %bias.5) | copy-start | bytes 27652
  19.8 3.8 %collective-permute-start.7 = (bf16[1,14,512]{2,1,0:T(8,128)(2,1)S(1)}, bf16[1,14,512]{2,1,0:T(8,128)(2,1)S(1)}, u32[]{:S(2)}, u32[]{:S(2)}) collective-permute-start(bf16[1,14,512]{2,1,0:T(8,128)(2,1)S(1)} %shard_map.78.feats), channel_id=1, source_target_pairs={{0,2},{2,0},{1,3},{3,1},{4,6},{6,4},{5,7},{7,5},{8,10},{10,8},{9,1... | collective-permute-start | bytes 43016 | tf_op jit(solution)/shard_map/ppermute | solution.py:24
  21.4 6.9 %collective-permute-start.9 = (bf16[14,2304]{1,0:T(8,128)(2,1)S(1)}, bf16[14,2304]{1,0:T(8,128)(2,1)S(1)}, u32[]{:S(2)}, u32[]{:S(2)}) collective-permute-start(bf16[14,2304]{1,0:T(8,128)(2,1)S(1)} %get-tuple-element.22.refs_2_), channel_id=1, source_target_pairs={{0,8},{4,12},{8,0},{12,4},{1,9},{5,13},{9,1},{13,5},{2,10},{6,14},... | collective-permute-start | bytes 193544 | tf_op jit(solution)/shard_map/ppermute | solution.py:29
  23.6 6.3 %collective-permute-start.8 = (bf16[14,2304]{1,0:T(8,128)(2,1)S(1)}, bf16[14,2304]{1,0:T(8,128)(2,1)S(1)}, u32[]{:S(2)}, u32[]{:S(2)}) collective-permute-start(bf16[14,2304]{1,0:T(8,128)(2,1)S(1)} %shard_map.80), channel_id=1, source_target_pairs={{0,12},{4,8},{8,4},{12,0},{1,13},{5,9},{9,5},{13,1},{2,14},{6,10},... | collective-permute-start | bytes 193544 | tf_op jit(solution)/shard_map/ppermute | solution.py:29
  26.2 4.5 %collective-permute-start.10 = (bf16[14,2304]{1,0:T(8,128)(2,1)S(1)}, bf16[14,2304]{1,0:T(8,128)(2,1)S(1)}, u32[]{:S(2)}, u32[]{:S(2)}) collective-permute-start(bf16[14,2304]{1,0:T(8,128)(2,1)S(1)} %get-tuple-element.24), channel_id=1, source_target_pairs={{0,4},{4,0},{8,12},{12,8},{1,5},{5,1},{9,13},{13,9},{2,6},{6,2},{1... | collective-permute-start | bytes 193544 | tf_op jit(solution)/shard_map/ppermute | solution.py:29

commit v5 on v4

--- a/solution.py
+++ b/solution.py
@@ -117,13 +117,13 @@
 
 
 def own_body(cores, feats, *refs):
-    decs, (out, x) = refs[:cores], refs[-2:]
+    decs, (out, x) = refs[:cores], refs[cores:]
     out[...] = dots(feats, decs, 0, x)
 
 
-def rest_body(cores, depth, slots, rows, base, bias, *refs):
+def rest_body(cores, depth, extra, slots, rows, base, bias, *refs):
     known, decs = refs[:depth], refs[depth : depth + cores]
-    outs, (total, x) = refs[depth + cores : -2], refs[-2:]
+    outs, (total, x) = refs[depth + cores + extra : -2], refs[-2:]
     total[...] = base[...]
     for k in range(depth):
 
@@ -186,7 +186,8 @@
     decs = [dec] + [rotated(dec_weight[0], "dec", j) for j in range(1, cores)]
     wide = cores * width
     parts = [None] * chips
-    before_encode = before_own = ()
+    before_encode = ()
+    groups = []
     direct = [k for k in range(chips) if k not in relayed]
     for slots in filter(None, (direct, relayed)):
         n = len(slots)
@@ -203,24 +204,28 @@
         base = call(
             functools.partial(own_body, cores),
             VMEM((n * SLOT, model), f32),
-            (VMEM,) * (1 + cores) + (any_,) * len(before_own),
-            [near(v) for v in (feats, *decs, *before_own)],
+            (VMEM,) * (1 + cores),
+            [near(v) for v in (feats, *decs)],
             (VMEM((n * SLOT, wide), bf16),),
             flops=2 * n * SLOT * model * wide,
             moved=wide * model * 2,
         )
+        before_encode = (base,)
+        groups.append((slots, known, base))
+    for g, (slots, known, base) in enumerate(groups):
+        n = len(slots)
+        later = tuple(other for _, _, other in groups[g + 1 :])
         outs = call(
-            functools.partial(rest_body, cores, depth, slots, rows),
+            functools.partial(rest_body, cores, depth, len(later), slots, rows),
             tuple(VMEM((rows, model), bf16 if k else f32) for k in slots),
-            (VMEM,) * (2 + depth + cores),
-            [near(v) for v in (base, dec_bias, *known, *decs)],
+            (VMEM,) * (2 + depth + cores) + (any_,) * len(later),
+            [near(v) for v in (base, dec_bias, *known, *decs, *later)],
             (VMEM((n * SLOT, model), f32), VMEM((n * SLOT, wide), bf16)),
             flops=2 * n * SLOT * model * wide * depth,
             moved=wide * model * 2 * depth,
         )
         for k, out in zip(slots, outs):
             parts[k] = out
-        before_encode, before_own = (base,), (outs[-1],)
     if relayed:
         parts[1], parts[-1] = lax.optimization_barrier((parts[1], parts[-1]))
     back = [paired(parts[k], "feat", k) for k in range(chips - 1, 0, -1)]

time: 31.5 us -> 31.6 us (level)
  starting transfers between devices: 14 us -> 13.6 us
  waiting for transfers between devices: 11.6 us -> 12 us
    ppermute x6, starting transfers between devices: 10.4 us -> 9.96 us  [paired(): return lax.ppermute(value, axis, [(i, i ^ by) for i in range(count)])]
    ppermute x5, waiting for transfers between devices: 1.19 us -> 1.61 us  [rotated(): lax.ppermute(value, axis, [(i, (i + by) % count) for i in range(count)])]
  transfers between devices with their start and end apart: 11 -> 11, of which waited for: 7 -> 8; matrix products, arithmetic and copies ran while one was open for 0% -> 0% of each run, Pallas kernels for 16% -> 16%
where the time goes in v5:
time: 31.6 us; the launch traced here: 31.4 us
  starting transfers between devices  13.6 us (43%)
  waiting for transfers between devices  12 us (38%)
  Pallas kernels  5.73 us (18%)
    ppermute x6, waiting for transfers between devices, paired(): return lax.ppermute(value, axis, [(i, i ^ by) for i in range(count)])  10.4 us
    ppermute x6, starting transfers between devices, paired(): return lax.ppermute(value, axis, [(i, i ^ by) for i in range(count)])  9.96 us
    pallas_call x9, Pallas kernels, call(): pl.pallas_call(body, out_shape=outs, in_specs=[pl.BlockSpec(memory_space=...  5.73 us
    ppermute x5, starting transfers between devices, rotated(): lax.ppermute(value, axis, [(i, (i + by) % count) for i in range(count)])  3.63 us
    ppermute x5, waiting for transfers between devices, rotated(): lax.ppermute(value, axis, [(i, (i + by) % count) for i in range(count)])  1.61 us
  transfers between devices with their start and end apart: 11, of which 8 were waited for; matrix products, arithmetic and copies ran while one was open for 0% of the time, Pallas kernels for 16%

profile of v5, /device:TPU:0, one launch (start us, length us, event | category | flops | bytes accessed | tf_op | source)
XLA Modules:
  0.0 31.4 jit_solution(13484118844384874537)
XLA Ops:
  0.0 0.5 %collective-permute-start.4 = (bf16[3,256,2304]{2,1,0:T(8,128)(2,1)}, bf16[3,256,2304]{2,1,0:T(8,128)(2,1)S(1)}, u32[]{:S(2)}, u32[]{:S(2)}) collective-permute-start(bf16[3,256,2304]{2,1,0:T(8,128)(2,1)} %bitcast.2), channel_id=1, source_target_pairs={{0,1},{1,0},{2,3},{3,2},{4,5},{5,4},{6,7},{7,6},{8,9},{9,8},{10,11... | collective-permute-start | bytes 10616840 | tf_op jit(solution)/shard_map/ppermute | solution.py:24
  0.5 0.1 collective-permute-start.3
  0.5 0.9 %shard_map.73.refs_0_ = bf16[2,14,2304]{2,1,0:T(8,128)(2,1)S(1)} custom-call(bf16[1,14,2304]{2,1,0:T(8,128)(2,1)} %clean.1, bf16[1,14,2304]{2,1,0:T(8,128)(2,1)} %corrupt.1), custom_call_target="tpu_custom_call" | custom-call | tf_op jit(solution)/shard_map/pallas_call | solution.py:41
  1.5 3.1 %collective-permute-start = (bf16[2,14,2304]{2,1,0:T(8,128)(2,1)S(1)}, bf16[2,14,2304]{2,1,0:T(8,128)(2,1)S(1)}, u32[]{:S(2)}, u32[]{:S(2)}) collective-permute-start(bf16[2,14,2304]{2,1,0:T(8,128)(2,1)S(1)} %shard_map.73.refs_0_), channel_id=1, source_target_pairs={{0,4},{4,0},{8,12},{12,8},{1,5},{5,1},{9,13},{13,9},{2,6},{6,2},{1... | collective-permute-start | bytes 387080 | tf_op jit(solution)/shard_map/ppermute | solution.py:29
  4.5 2.6 %collective-permute-start.1 = (bf16[2,14,2304]{2,1,0:T(8,128)(2,1)S(1)}, bf16[2,14,2304]{2,1,0:T(8,128)(2,1)S(1)}, u32[]{:S(2)}, u32[]{:S(2)}) collective-permute-start(bf16[2,14,2304]{2,1,0:T(8,128)(2,1)S(1)} %shard_map.73.refs_0_), channel_id=1, source_target_pairs={{0,8},{4,12},{8,0},{12,4},{1,9},{5,13},{9,1},{13,5},{2,10},{6,14},... | collective-permute-start | bytes 387080 | tf_op jit(solution)/shard_map/ppermute | solution.py:29
  7.1 4.2 %collective-permute-done.after.refs_1_ = bf16[2,14,2304]{2,1,0:T(8,128)(2,1)S(1)} collective-permute-done((bf16[2,14,2304]{2,1,0:T(8,128)(2,1)S(1)}, bf16[2,14,2304]{2,1,0:T(8,128)(2,1)S(1)}, u32[]{:S(2)}, u32[]{:S(2)}) %collective-permute-start) | collective-permute-done | bytes 129056 | tf_op jit(solution)/shard_map/ppermute | solution.py:29
  11.3 2.0 %shard_map.74 = (bf16[2304,256]{1,0:T(8,128)(2,1)S(1)}, bf16[2,256,2304]{2,1,0:T(8,128)(2,1)S(1)}, f32[2,256]{1,0:T(2,128)S(1)}) custom-call(bf16[1,2304,256]{2,1,0:T(8,128)(2,1)} %enc.1, bf16[1,3,256,2304]{3,2,1,0:T(8,128)(2,1)} %dec.1, f32[1,256]{1,0:T(1,128)} %bias.3, s32[1,1,16]{2,1,0:T(1,128)} %picks.1, ...), custom_call_target="tpu_custom_call" | custom-call | tf_op jit(solution)/shard_map/pallas_call | solution.py:41
  13.3 0.8 %collective-permute-done.1.refs_2_ = bf16[2,14,2304]{2,1,0:T(8,128)(2,1)S(1)} collective-permute-done((bf16[2,14,2304]{2,1,0:T(8,128)(2,1)S(1)}, bf16[2,14,2304]{2,1,0:T(8,128)(2,1)S(1)}, u32[]{:S(2)}, u32[]{:S(2)}) %collective-permute-start.1) | collective-permute-done | bytes 129056 | tf_op jit(solution)/shard_map/ppermute | solution.py:29
  14.1 0.4 %collective-permute-start.6 = (bf16[2,14,2304]{2,1,0:T(8,128)(2,1)S(1)}, bf16[2,14,2304]{2,1,0:T(8,128)(2,1)S(1)}, u32[]{:S(2)}, u32[]{:S(2)}) collective-permute-start(bf16[2,14,2304]{2,1,0:T(8,128)(2,1)S(1)} %collective-permute-done.1.refs_2_), channel_id=1, source_target_pairs={{0,4},{4,0},{8,12},{12,8},{1,5},{5,1},{9,13},{13,9},{2,6},{6,2},{1... | collective-permute-start | bytes 387080 | tf_op jit(solution)/shard_map/ppermute | solution.py:29
  14.6 0.0 collective-permute-start.2
  14.6 1.2 %collective-permute-done.2.refs_4_.refs_3_ = f32[2,256]{1,0:T(2,128)S(1)} collective-permute-done((f32[2,256]{1,0:T(2,128)S(1)}, f32[2,256]{1,0:T(2,128)S(1)}, u32[]{:S(2)}, u32[]{:S(2)}) %collective-permute-start.2) | collective-permute-done | bytes 2080 | tf_op jit(solution)/shard_map/ppermute | solution.py:24
  15.7 0.0 collective-permute-done.3.refs_6_.refs_5_
  15.7 0.5 %shard_map.75.feats = bf16[3,14,512]{2,1,0:T(8,128)(2,1)S(1)} custom-call(bf16[2,14,2304]{2,1,0:T(8,128)(2,1)S(1)} %shard_map.73.refs_0_, bf16[2,14,2304]{2,1,0:T(8,128)(2,1)S(1)} %collective-permute-done.after.refs_1_, bf16[2,14,2304]{2,1,0:T(8,128)(2,1)S(1)} %collective-permute-done.1.refs_2_, f32[2,256]{1,0:T(2,128)S(1)} %get-tuple-element.17.refs_3_.refs_2_, ...), custom_call_target="tpu_custom_call" | custom-call | flops 226492416 | bytes 2359296 | tf_op jit(solution)/shard_map/pallas_call | solution.py:41
  16.3 1.6 %collective-permute-start.5 = (bf16[3,14,512]{2,1,0:T(8,128)(2,1)S(1)}, bf16[3,14,512]{2,1,0:T(8,128)(2,1)S(1)}, u32[]{:S(2)}, u32[]{:S(2)}) collective-permute-start(bf16[3,14,512]{2,1,0:T(8,128)(2,1)S(1)} %shard_map.75.feats), channel_id=1, source_target_pairs={{0,2},{2,0},{1,3},{3,1},{4,6},{6,4},{5,7},{7,5},{8,10},{10,8},{9,1... | collective-permute-start | bytes 129032 | tf_op jit(solution)/shard_map/ppermute | solution.py:24
  17.8 0.0 collective-permute-done.4.refs_1_.refs_2_
  17.8 0.5 %shard_map.76.refs_0_.base = f32[48,2304]{1,0:T(8,128)S(1)} custom-call(bf16[3,14,512]{2,1,0:T(8,128)(2,1)S(1)} %shard_map.75.feats, bf16[2,256,2304]{2,1,0:T(8,128)(2,1)S(1)} %get-tuple-element.19.refs_0_.refs_1_, bf16[3,256,2304]{2,1,0:T(8,128)(2,1)S(1)} %collective-permute-done.4.refs_1_.refs_2_), custom_call_target="tpu_custom_call" | custom-call | flops 113246208 | bytes 2359296 | tf_op jit(solution)/shard_map/pallas_call | solution.py:41
  18.4 0.9 %collective-permute-done.6.refs_1_ = bf16[2,14,2304]{2,1,0:T(8,128)(2,1)S(1)} collective-permute-done((bf16[2,14,2304]{2,1,0:T(8,128)(2,1)S(1)}, bf16[2,14,2304]{2,1,0:T(8,128)(2,1)S(1)}, u32[]{:S(2)}, u32[]{:S(2)}) %collective-permute-start.6) | collective-permute-done | bytes 129056 | tf_op jit(solution)/shard_map/ppermute | solution.py:29
  19.3 0.5 %shard_map.77.feats = bf16[1,14,512]{2,1,0:T(8,128)(2,1)S(1)} custom-call(f32[48,2304]{1,0:T(8,128)S(1)} %shard_map.76.refs_0_.base, bf16[2,14,2304]{2,1,0:T(8,128)(2,1)S(1)} %collective-permute-done.6.refs_1_, f32[2,256]{1,0:T(2,128)S(1)} %get-tuple-element.17.refs_3_.refs_2_, f32[2,256]{1,0:T(2,128)S(1)} %collective-permute-done.2.refs_4_.refs_3_, ...), custom_call_target="tpu_custom_call" | custom-call | flops 75497472 | bytes 2359296 | tf_op jit(solution)/shard_map/pallas_call | solution.py:41
  19.8 0.0 copy-start
  19.8 1.6 %collective-permute-start.7 = (bf16[1,14,512]{2,1,0:T(8,128)(2,1)S(1)}, bf16[1,14,512]{2,1,0:T(8,128)(2,1)S(1)}, u32[]{:S(2)}, u32[]{:S(2)}) collective-permute-start(bf16[1,14,512]{2,1,0:T(8,128)(2,1)S(1)} %shard_map.77.feats), channel_id=1, source_target_pairs={{0,2},{2,0},{1,3},{3,1},{4,6},{6,4},{5,7},{7,5},{8,10},{10,8},{9,1... | collective-permute-start | bytes 43016 | tf_op jit(solution)/shard_map/ppermute | solution.py:24
  21.4 0.4 %shard_map.78.refs_3_.base = f32[16,2304]{1,0:T(8,128)S(1)} custom-call(bf16[1,14,512]{2,1,0:T(8,128)(2,1)S(1)} %shard_map.77.feats, bf16[2,256,2304]{2,1,0:T(8,128)(2,1)S(1)} %get-tuple-element.19.refs_0_.refs_1_, bf16[3,256,2304]{2,1,0:T(8,128)(2,1)S(1)} %collective-permute-done.4.refs_1_.refs_2_), custom_call_target="tpu_custom_call" | custom-call | flops 37748736 | bytes 2359296 | tf_op jit(solution)/shard_map/pallas_call | solution.py:41
  21.8 0.0 collective-permute-done.5.refs_0_
  21.8 0.0 copy-done
  21.8 0.1 shard_map.79
  21.9 1.3 %collective-permute-start.9 = (bf16[14,2304]{1,0:T(8,128)(2,1)S(1)}, bf16[14,2304]{1,0:T(8,128)(2,1)S(1)}, u32[]{:S(2)}, u32[]{:S(2)}) collective-permute-start(bf16[14,2304]{1,0:T(8,128)(2,1)S(1)} %get-tuple-element.23), channel_id=1, source_target_pairs={{0,8},{4,12},{8,0},{12,4},{1,9},{5,13},{9,1},{13,5},{2,10},{6,14},... | collective-permute-start | bytes 193544 | tf_op jit(solution)/shard_map/ppermute | solution.py:29
  23.2 0.5 %collective-permute-done.7.refs_0_ = bf16[1,14,512]{2,1,0:T(8,128)(2,1)S(1)} collective-permute-done((bf16[1,14,512]{2,1,0:T(8,128)(2,1)S(1)}, bf16[1,14,512]{2,1,0:T(8,128)(2,1)S(1)}, u32[]{:S(2)}, u32[]{:S(2)}) %collective-permute-start.7) | collective-permute-done | bytes 14368 | tf_op jit(solution)/shard_map/ppermute | solution.py:24
  23.6 2.5 %collective-permute-start.8 = (bf16[14,2304]{1,0:T(8,128)(2,1)S(1)}, bf16[14,2304]{1,0:T(8,128)(2,1)S(1)}, u32[]{:S(2)}, u32[]{:S(2)}) collective-permute-start(bf16[14,2304]{1,0:T(8,128)(2,1)S(1)} %shard_map.80), channel_id=1, source_target_pairs={{0,12},{4,8},{8,4},{12,0},{1,13},{5,9},{9,5},{13,1},{2,14},{6,10},... | collective-permute-start | bytes 193544 | tf_op jit(solution)/shard_map/ppermute | solution.py:29
  26.2 0.0 collective-permute-start.10
  26.2 2.5 %collective-permute-done.9.refs_1_ = bf16[14,2304]{1,0:T(8,128)(2,1)S(1)} collective-permute-done((bf16[14,2304]{1,0:T(8,128)(2,1)S(1)}, bf16[14,2304]{1,0:T(8,128)(2,1)S(1)}, u32[]{:S(2)}, u32[]{:S(2)}) %collective-permute-start.9) | collective-permute-done | bytes 64544 | tf_op jit(solution)/shard_map/ppermute | solution.py:29
  28.6 1.3 %collective-permute-done.8.refs_0_ = bf16[14,2304]{1,0:T(8,128)(2,1)S(1)} collective-permute-done((bf16[14,2304]{1,0:T(8,128)(2,1)S(1)}, bf16[14,2304]{1,0:T(8,128)(2,1)S(1)}, u32[]{:S(2)}, u32[]{:S(2)}) %collective-permute-start.8) | collective-permute-done | bytes 64544 | tf_op jit(solution)/shard_map/ppermute | solution.py:29
  30.0 0.8 %collective-permute-done.10.refs_2_ = bf16[14,2304]{1,0:T(8,128)(2,1)S(1)} collective-permute-done((bf16[14,2304]{1,0:T(8,128)(2,1)S(1)}, bf16[14,2304]{1,0:T(8,128)(2,1)S(1)}, u32[]{:S(2)}, u32[]{:S(2)}) %collective-permute-start.10) | collective-permute-done | bytes 64544 | tf_op jit(solution)/shard_map/ppermute | solution.py:29
  30.8 0.7 %shard_map.81 = bf16[1,14,2304]{2,1,0:T(8,128)(2,1)} custom-call(f32[14,2304]{1,0:T(8,128)S(1)} %get-tuple-element.20.own, bf16[14,2304]{1,0:T(8,128)(2,1)S(1)} %collective-permute-done.8.refs_0_, bf16[14,2304]{1,0:T(8,128)(2,1)S(1)} %collective-permute-done.9.refs_1_, bf16[14,2304]{1,0:T(8,128)(2,1)S(1)} %collective-permute-done.10.refs_2_), custom_call_target="tpu_custom_call" | custom-call | tf_op jit(solution)/shard_map/pallas_call | solution.py:41
  (1 shorter events, 0.0 us)
Async XLA Ops:
  0.0 17.8 %collective-permute-start.4 = (bf16[3,256,2304]{2,1,0:T(8,128)(2,1)}, bf16[3,256,2304]{2,1,0:T(8,128)(2,1)S(1)}, u32[]{:S(2)}, u32[]{:S(2)}) collective-permute-start(bf16[3,256,2304]{2,1,0:T(8,128)(2,1)} %bitcast.2), channel_id=1, source_target_pairs={{0,1},{1,0},{2,3},{3,2},{4,5},{5,4},{6,7},{7,6},{8,9},{9,8},{10,11... | collective-permute-start | bytes 10616840 | tf_op jit(solution)/shard_map/ppermute | solution.py:24
  0.5 15.3 %collective-permute-start.3 = (bf16[2304,256]{1,0:T(8,128)(2,1)}, bf16[2304,256]{1,0:T(8,128)(2,1)S(1)}, u32[]{:S(2)}, u32[]{:S(2)}) collective-permute-start(bf16[2304,256]{1,0:T(8,128)(2,1)} %bitcast.3), channel_id=1, source_target_pairs={{0,1},{1,0},{2,3},{3,2},{4,5},{5,4},{6,7},{7,6},{8,9},{9,8},{10,11... | collective-permute-start | bytes 3538952 | tf_op jit(solution)/shard_map/ppermute | solution.py:24
  1.5 9.8 %collective-permute-start = (bf16[2,14,2304]{2,1,0:T(8,128)(2,1)S(1)}, bf16[2,14,2304]{2,1,0:T(8,128)(2,1)S(1)}, u32[]{:S(2)}, u32[]{:S(2)}) collective-permute-start(bf16[2,14,2304]{2,1,0:T(8,128)(2,1)S(1)} %shard_map.73.refs_0_), channel_id=1, source_target_pairs={{0,4},{4,0},{8,12},{12,8},{1,5},{5,1},{9,13},{13,9},{2,6},{6,2},{1... | collective-permute-start | bytes 387080 | tf_op jit(solution)/shard_map/ppermute | solution.py:29
  4.5 9.6 %collective-permute-start.1 = (bf16[2,14,2304]{2,1,0:T(8,128)(2,1)S(1)}, bf16[2,14,2304]{2,1,0:T(8,128)(2,1)S(1)}, u32[]{:S(2)}, u32[]{:S(2)}) collective-permute-start(bf16[2,14,2304]{2,1,0:T(8,128)(2,1)S(1)} %shard_map.73.refs_0_), channel_id=1, source_target_pairs={{0,8},{4,12},{8,0},{12,4},{1,9},{5,13},{9,1},{13,5},{2,10},{6,14},... | collective-permute-start | bytes 387080 | tf_op jit(solution)/shard_map/ppermute | solution.py:29
  14.1 5.1 %collective-permute-start.6 = (bf16[2,14,2304]{2,1,0:T(8,128)(2,1)S(1)}, bf16[2,14,2304]{2,1,0:T(8,128)(2,1)S(1)}, u32[]{:S(2)}, u32[]{:S(2)}) collective-permute-start(bf16[2,14,2304]{2,1,0:T(8,128)(2,1)S(1)} %collective-permute-done.1.refs_2_), channel_id=1, source_target_pairs={{0,4},{4,0},{8,12},{12,8},{1,5},{5,1},{9,13},{13,9},{2,6},{6,2},{1... | collective-permute-start | bytes 387080 | tf_op jit(solution)/shard_map/ppermute | solution.py:29
  14.6 1.2 %collective-permute-start.2 = (f32[2,256]{1,0:T(2,128)S(1)}, f32[2,256]{1,0:T(2,128)S(1)}, u32[]{:S(2)}, u32[]{:S(2)}) collective-permute-start(f32[2,256]{1,0:T(2,128)S(1)} %get-tuple-element.17.refs_3_.refs_2_), channel_id=1, source_target_pairs={{0,1},{1,0},{2,3},{3,2},{4,5},{5,4},{6,7},{7,6},{8,9},{9,8},{10,11... | collective-permute-start | bytes 6152 | tf_op jit(solution)/shard_map/ppermute | solution.py:24
  16.3 5.5 %collective-permute-start.5 = (bf16[3,14,512]{2,1,0:T(8,128)(2,1)S(1)}, bf16[3,14,512]{2,1,0:T(8,128)(2,1)S(1)}, u32[]{:S(2)}, u32[]{:S(2)}) collective-permute-start(bf16[3,14,512]{2,1,0:T(8,128)(2,1)S(1)} %shard_map.75.feats), channel_id=1, source_target_pairs={{0,2},{2,0},{1,3},{3,1},{4,6},{6,4},{5,7},{7,5},{8,10},{10,8},{9,1... | collective-permute-start | bytes 129032 | tf_op jit(solution)/shard_map/ppermute | solution.py:24
  19.8 2.0 %copy-start = (f32[1,2304]{1,0:T(1,128)S(1)}, f32[1,2304]{1,0:T(1,128)}, u32[]{:S(2)}) copy-start(f32[1,2304]{1,0:T(1,128)} %bias.5) | copy-start | bytes 27652
  19.8 3.8 %collective-permute-start.7 = (bf16[1,14,512]{2,1,0:T(8,128)(2,1)S(1)}, bf16[1,14,512]{2,1,0:T(8,128)(2,1)S(1)}, u32[]{:S(2)}, u32[]{:S(2)}) collective-permute-start(bf16[1,14,512]{2,1,0:T(8,128)(2,1)S(1)} %shard_map.77.feats), channel_id=1, source_target_pairs={{0,2},{2,0},{1,3},{3,1},{4,6},{6,4},{5,7},{7,5},{8,10},{10,8},{9,1... | collective-permute-start | bytes 43016 | tf_op jit(solution)/shard_map/ppermute | solution.py:24
  21.9 6.8 %collective-permute-start.9 = (bf16[14,2304]{1,0:T(8,128)(2,1)S(1)}, bf16[14,2304]{1,0:T(8,128)(2,1)S(1)}, u32[]{:S(2)}, u32[]{:S(2)}) collective-permute-start(bf16[14,2304]{1,0:T(8,128)(2,1)S(1)} %get-tuple-element.23), channel_id=1, source_target_pairs={{0,8},{4,12},{8,0},{12,4},{1,9},{5,13},{9,1},{13,5},{2,10},{6,14},... | collective-permute-start | bytes 193544 | tf_op jit(solution)/shard_map/ppermute | solution.py:29
  23.6 6.3 %collective-permute-start.8 = (bf16[14,2304]{1,0:T(8,128)(2,1)S(1)}, bf16[14,2304]{1,0:T(8,128)(2,1)S(1)}, u32[]{:S(2)}, u32[]{:S(2)}) collective-permute-start(bf16[14,2304]{1,0:T(8,128)(2,1)S(1)} %shard_map.80), channel_id=1, source_target_pairs={{0,12},{4,8},{8,4},{12,0},{1,13},{5,9},{9,5},{13,1},{2,14},{6,10},... | collective-permute-start | bytes 193544 | tf_op jit(solution)/shard_map/ppermute | solution.py:29
  26.2 4.6 %collective-permute-start.10 = (bf16[14,2304]{1,0:T(8,128)(2,1)S(1)}, bf16[14,2304]{1,0:T(8,128)(2,1)S(1)}, u32[]{:S(2)}, u32[]{:S(2)}) collective-permute-start(bf16[14,2304]{1,0:T(8,128)(2,1)S(1)} %get-tuple-element.24), channel_id=1, source_target_pairs={{0,4},{4,0},{8,12},{12,8},{1,5},{5,1},{9,13},{13,9},{2,6},{6,2},{1... | collective-permute-start | bytes 193544 | tf_op jit(solution)/shard_map/ppermute | solution.py:29

commit v6 on v5

--- a/solution.py
+++ b/solution.py
@@ -161,6 +161,7 @@
     )
     relayed = [k for k in range(2, chips) if k % 2]
     got = [both] + [None if k in relayed else paired(both, "feat", k) for k in range(1, chips)]
+    swapped = [rotated(enc_weight[0], "dec", j) for j in range(1, cores)]
     enc, dec, small = call(
         functools.partial(load_body, depth + 1),
         (
@@ -169,7 +170,7 @@
             VMEM((2, width), f32),
         ),
         (hbm,) * 4 + (any_,),
-        [far(v) for v in (enc_weight, dec_weight, enc_bias, patch_index)] + [got[1]],
+        [far(v) for v in (enc_weight, dec_weight, enc_bias, patch_index)] + [swapped[0]],
         (
             VMEM((1, width), f32),
             pltpu.SMEM(patch_index.shape[1:], jnp.int32),
@@ -182,7 +183,7 @@
             got[k - 1] = v
             got[k] = paired(v, "feat", 1)
     smalls = [small] + [rotated(small, "dec", j) for j in range(1, cores)]
-    encs = [enc] + [rotated(enc_weight[0], "dec", j) for j in range(1, cores)]
+    encs = [enc] + swapped
     decs = [dec] + [rotated(dec_weight[0], "dec", j) for j in range(1, cores)]
     wide = cores * width
     parts = [None] * chips

time: 31.6 us -> 31.7 us (level)
  starting transfers between devices: 13.6 us -> 15.8 us
  waiting for transfers between devices: 12 us -> 9.9 us
    ppermute x6, waiting for transfers between devices: 10.4 us -> 7.68 us  [paired(): return lax.ppermute(value, axis, [(i, i ^ by) for i in range(count)])]
    ppermute x6, starting transfers between devices: 9.96 us -> 12.1 us  [paired(): return lax.ppermute(value, axis, [(i, i ^ by) for i in range(count)])]
    ppermute x5, waiting for transfers between devices: 1.61 us -> 2.22 us  [rotated(): lax.ppermute(value, axis, [(i, (i + by) % count) for i in range(count)])]
  transfers between devices with their start and end apart: 11 -> 11, of which waited for: 8 -> 6; matrix products, arithmetic and copies ran while one was open for 0% -> 0% of each run, Pallas kernels for 16% -> 16%
where the time goes in v6:
time: 31.7 us; the launch traced here: 31.5 us
  starting transfers between devices  15.8 us (50%)
  waiting for transfers between devices  9.9 us (31%)
  Pallas kernels  5.74 us (18%)
    ppermute x6, starting transfers between devices, paired(): return lax.ppermute(value, axis, [(i, i ^ by) for i in range(count)])  12.1 us
    ppermute x6, waiting for transfers between devices, paired(): return lax.ppermute(value, axis, [(i, i ^ by) for i in range(count)])  7.68 us
    pallas_call x9, Pallas kernels, call(): pl.pallas_call(body, out_shape=outs, in_specs=[pl.BlockSpec(memory_space=...  5.74 us
    ppermute x5, starting transfers between devices, rotated(): lax.ppermute(value, axis, [(i, (i + by) % count) for i in range(count)])  3.68 us
    ppermute x5, waiting for transfers between devices, rotated(): lax.ppermute(value, axis, [(i, (i + by) % count) for i in range(count)])  2.22 us
  transfers between devices with their start and end apart: 11, of which 6 were waited for; matrix products, arithmetic and copies ran while one was open for 0% of the time, Pallas kernels for 16%

profile of v6, /device:TPU:0, one launch (start us, length us, event | category | flops | bytes accessed | tf_op | source)
XLA Modules:
  0.0 31.5 jit_solution(1343814398750590529)
XLA Ops:
  0.0 0.5 %collective-permute-start.4 = (bf16[3,256,2304]{2,1,0:T(8,128)(2,1)}, bf16[3,256,2304]{2,1,0:T(8,128)(2,1)S(1)}, u32[]{:S(2)}, u32[]{:S(2)}) collective-permute-start(bf16[3,256,2304]{2,1,0:T(8,128)(2,1)} %bitcast.2), channel_id=1, source_target_pairs={{0,1},{1,0},{2,3},{3,2},{4,5},{5,4},{6,7},{7,6},{8,9},{9,8},{10,11... | collective-permute-start | bytes 10616840 | tf_op jit(solution)/shard_map/ppermute | solution.py:24
  0.5 0.1 collective-permute-start.2
  0.5 0.9 %shard_map.73.refs_0_ = bf16[2,14,2304]{2,1,0:T(8,128)(2,1)S(1)} custom-call(bf16[1,14,2304]{2,1,0:T(8,128)(2,1)} %clean.1, bf16[1,14,2304]{2,1,0:T(8,128)(2,1)} %corrupt.1), custom_call_target="tpu_custom_call" | custom-call | tf_op jit(solution)/shard_map/pallas_call | solution.py:41
  1.5 4.1 %collective-permute-start.1 = (bf16[2,14,2304]{2,1,0:T(8,128)(2,1)S(1)}, bf16[2,14,2304]{2,1,0:T(8,128)(2,1)S(1)}, u32[]{:S(2)}, u32[]{:S(2)}) collective-permute-start(bf16[2,14,2304]{2,1,0:T(8,128)(2,1)S(1)} %shard_map.73.refs_0_), channel_id=1, source_target_pairs={{0,8},{4,12},{8,0},{12,4},{1,9},{5,13},{9,1},{13,5},{2,10},{6,14},... | collective-permute-start | bytes 387080 | tf_op jit(solution)/shard_map/ppermute | solution.py:29
  5.6 1.6 %collective-permute-start = (bf16[2,14,2304]{2,1,0:T(8,128)(2,1)S(1)}, bf16[2,14,2304]{2,1,0:T(8,128)(2,1)S(1)}, u32[]{:S(2)}, u32[]{:S(2)}) collective-permute-start(bf16[2,14,2304]{2,1,0:T(8,128)(2,1)S(1)} %shard_map.73.refs_0_), channel_id=1, source_target_pairs={{0,4},{4,0},{8,12},{12,8},{1,5},{5,1},{9,13},{13,9},{2,6},{6,2},{1... | collective-permute-start | bytes 387080 | tf_op jit(solution)/shard_map/ppermute | solution.py:29
  7.1 1.1 %collective-permute-done.2.after.refs_6_.refs_5_ = bf16[2304,256]{1,0:T(8,128)(2,1)S(1)} collective-permute-done((bf16[2304,256]{1,0:T(8,128)(2,1)}, bf16[2304,256]{1,0:T(8,128)(2,1)S(1)}, u32[]{:S(2)}, u32[]{:S(2)}) %collective-permute-start.2) | collective-permute-done | bytes 1179680 | tf_op jit(solution)/shard_map/ppermute | solution.py:24
  8.2 2.0 %shard_map.74 = (bf16[2304,256]{1,0:T(8,128)(2,1)S(1)}, bf16[2,256,2304]{2,1,0:T(8,128)(2,1)S(1)}, f32[2,256]{1,0:T(2,128)S(1)}) custom-call(bf16[1,2304,256]{2,1,0:T(8,128)(2,1)} %enc.1, bf16[1,3,256,2304]{3,2,1,0:T(8,128)(2,1)} %dec.1, f32[1,256]{1,0:T(1,128)} %bias.3, s32[1,1,16]{2,1,0:T(1,128)} %picks.1, ...), custom_call_target="tpu_custom_call" | custom-call | tf_op jit(solution)/shard_map/pallas_call | solution.py:41
  10.2 2.6 %collective-permute-done.1.refs_2_ = bf16[2,14,2304]{2,1,0:T(8,128)(2,1)S(1)} collective-permute-done((bf16[2,14,2304]{2,1,0:T(8,128)(2,1)S(1)}, bf16[2,14,2304]{2,1,0:T(8,128)(2,1)S(1)}, u32[]{:S(2)}, u32[]{:S(2)}) %collective-permute-start.1) | collective-permute-done | bytes 129056 | tf_op jit(solution)/shard_map/ppermute | solution.py:29
  12.8 0.6 %collective-permute-start.6 = (bf16[2,14,2304]{2,1,0:T(8,128)(2,1)S(1)}, bf16[2,14,2304]{2,1,0:T(8,128)(2,1)S(1)}, u32[]{:S(2)}, u32[]{:S(2)}) collective-permute-start(bf16[2,14,2304]{2,1,0:T(8,128)(2,1)S(1)} %collective-permute-done.1.refs_2_), channel_id=1, source_target_pairs={{0,4},{4,0},{8,12},{12,8},{1,5},{5,1},{9,13},{13,9},{2,6},{6,2},{1... | collective-permute-start | bytes 387080 | tf_op jit(solution)/shard_map/ppermute | solution.py:29
  13.5 0.0 collective-permute-start.3
  13.5 0.0 collective-permute-done.refs_1_
  13.5 1.2 %collective-permute-done.3.refs_4_.refs_3_ = f32[2,256]{1,0:T(2,128)S(1)} collective-permute-done((f32[2,256]{1,0:T(2,128)S(1)}, f32[2,256]{1,0:T(2,128)S(1)}, u32[]{:S(2)}, u32[]{:S(2)}) %collective-permute-start.3) | collective-permute-done | bytes 2080 | tf_op jit(solution)/shard_map/ppermute | solution.py:24
  14.6 0.5 %shard_map.75.feats = bf16[3,14,512]{2,1,0:T(8,128)(2,1)S(1)} custom-call(bf16[2,14,2304]{2,1,0:T(8,128)(2,1)S(1)} %shard_map.73.refs_0_, bf16[2,14,2304]{2,1,0:T(8,128)(2,1)S(1)} %collective-permute-done.refs_1_, bf16[2,14,2304]{2,1,0:T(8,128)(2,1)S(1)} %collective-permute-done.1.refs_2_, f32[2,256]{1,0:T(2,128)S(1)} %get-tuple-element.17.refs_3_.refs_2_, ...), custom_call_target="tpu_custom_call" | custom-call | flops 226492416 | bytes 2359296 | tf_op jit(solution)/shard_map/pallas_call | solution.py:41
  15.2 1.6 %collective-permute-start.5 = (bf16[3,14,512]{2,1,0:T(8,128)(2,1)S(1)}, bf16[3,14,512]{2,1,0:T(8,128)(2,1)S(1)}, u32[]{:S(2)}, u32[]{:S(2)}) collective-permute-start(bf16[3,14,512]{2,1,0:T(8,128)(2,1)S(1)} %shard_map.75.feats), channel_id=1, source_target_pairs={{0,2},{2,0},{1,3},{3,1},{4,6},{6,4},{5,7},{7,5},{8,10},{10,8},{9,1... | collective-permute-start | bytes 129032 | tf_op jit(solution)/shard_map/ppermute | solution.py:24
  16.7 0.0 collective-permute-done.4.refs_1_.refs_2_
  16.7 0.5 %shard_map.76.refs_0_.base = f32[48,2304]{1,0:T(8,128)S(1)} custom-call(bf16[3,14,512]{2,1,0:T(8,128)(2,1)S(1)} %shard_map.75.feats, bf16[2,256,2304]{2,1,0:T(8,128)(2,1)S(1)} %get-tuple-element.19.refs_0_.refs_1_, bf16[3,256,2304]{2,1,0:T(8,128)(2,1)S(1)} %collective-permute-done.4.refs_1_.refs_2_), custom_call_target="tpu_custom_call" | custom-call | flops 113246208 | bytes 2359296 | tf_op jit(solution)/shard_map/pallas_call | solution.py:41
  17.2 0.7 %collective-permute-done.6.refs_1_ = bf16[2,14,2304]{2,1,0:T(8,128)(2,1)S(1)} collective-permute-done((bf16[2,14,2304]{2,1,0:T(8,128)(2,1)S(1)}, bf16[2,14,2304]{2,1,0:T(8,128)(2,1)S(1)}, u32[]{:S(2)}, u32[]{:S(2)}) %collective-permute-start.6) | collective-permute-done | bytes 129056 | tf_op jit(solution)/shard_map/ppermute | solution.py:29
  18.0 0.5 %shard_map.77.feats = bf16[1,14,512]{2,1,0:T(8,128)(2,1)S(1)} custom-call(f32[48,2304]{1,0:T(8,128)S(1)} %shard_map.76.refs_0_.base, bf16[2,14,2304]{2,1,0:T(8,128)(2,1)S(1)} %collective-permute-done.6.refs_1_, f32[2,256]{1,0:T(2,128)S(1)} %get-tuple-element.17.refs_3_.refs_2_, f32[2,256]{1,0:T(2,128)S(1)} %collective-permute-done.3.refs_4_.refs_3_, ...), custom_call_target="tpu_custom_call" | custom-call | flops 75497472 | bytes 2359296 | tf_op jit(solution)/shard_map/pallas_call | solution.py:41
  18.5 0.0 copy-start
  18.5 1.6 %collective-permute-start.7 = (bf16[1,14,512]{2,1,0:T(8,128)(2,1)S(1)}, bf16[1,14,512]{2,1,0:T(8,128)(2,1)S(1)}, u32[]{:S(2)}, u32[]{:S(2)}) collective-permute-start(bf16[1,14,512]{2,1,0:T(8,128)(2,1)S(1)} %shard_map.77.feats), channel_id=1, source_target_pairs={{0,2},{2,0},{1,3},{3,1},{4,6},{6,4},{5,7},{7,5},{8,10},{10,8},{9,1... | collective-permute-start | bytes 43016 | tf_op jit(solution)/shard_map/ppermute | solution.py:24
  20.1 0.4 %shard_map.78.refs_3_.base = f32[16,2304]{1,0:T(8,128)S(1)} custom-call(bf16[1,14,512]{2,1,0:T(8,128)(2,1)S(1)} %shard_map.77.feats, bf16[2,256,2304]{2,1,0:T(8,128)(2,1)S(1)} %get-tuple-element.19.refs_0_.refs_1_, bf16[3,256,2304]{2,1,0:T(8,128)(2,1)S(1)} %collective-permute-done.4.refs_1_.refs_2_), custom_call_target="tpu_custom_call" | custom-call | flops 37748736 | bytes 2359296 | tf_op jit(solution)/shard_map/pallas_call | solution.py:41
  20.5 0.0 collective-permute-done.5.refs_0_
  20.5 0.0 copy-done
  20.5 0.1 shard_map.79
  20.6 2.9 %collective-permute-start.9 = (bf16[14,2304]{1,0:T(8,128)(2,1)S(1)}, bf16[14,2304]{1,0:T(8,128)(2,1)S(1)}, u32[]{:S(2)}, u32[]{:S(2)}) collective-permute-start(bf16[14,2304]{1,0:T(8,128)(2,1)S(1)} %get-tuple-element.23), channel_id=1, source_target_pairs={{0,8},{4,12},{8,0},{12,4},{1,9},{5,13},{9,1},{13,5},{2,10},{6,14},... | collective-permute-start | bytes 193544 | tf_op jit(solution)/shard_map/ppermute | solution.py:29
  23.5 0.0 collective-permute-done.7.refs_0_
  23.6 2.9 %collective-permute-start.8 = (bf16[14,2304]{1,0:T(8,128)(2,1)S(1)}, bf16[14,2304]{1,0:T(8,128)(2,1)S(1)}, u32[]{:S(2)}, u32[]{:S(2)}) collective-permute-start(bf16[14,2304]{1,0:T(8,128)(2,1)S(1)} %shard_map.80), channel_id=1, source_target_pairs={{0,12},{4,8},{8,4},{12,0},{1,13},{5,9},{9,5},{13,1},{2,14},{6,10},... | collective-permute-start | bytes 193544 | tf_op jit(solution)/shard_map/ppermute | solution.py:29
  26.5 0.0 collective-permute-start.10
  26.5 0.0 collective-permute-done.9.refs_1_
  26.5 3.4 %collective-permute-done.8.refs_0_ = bf16[14,2304]{1,0:T(8,128)(2,1)S(1)} collective-permute-done((bf16[14,2304]{1,0:T(8,128)(2,1)S(1)}, bf16[14,2304]{1,0:T(8,128)(2,1)S(1)}, u32[]{:S(2)}, u32[]{:S(2)}) %collective-permute-start.8) | collective-permute-done | bytes 64544 | tf_op jit(solution)/shard_map/ppermute | solution.py:29
  29.9 1.0 %collective-permute-done.10.refs_2_ = bf16[14,2304]{1,0:T(8,128)(2,1)S(1)} collective-permute-done((bf16[14,2304]{1,0:T(8,128)(2,1)S(1)}, bf16[14,2304]{1,0:T(8,128)(2,1)S(1)}, u32[]{:S(2)}, u32[]{:S(2)}) %collective-permute-start.10) | collective-permute-done | bytes 64544 | tf_op jit(solution)/shard_map/ppermute | solution.py:29
  30.8 0.7 %shard_map.81 = bf16[1,14,2304]{2,1,0:T(8,128)(2,1)} custom-call(f32[14,2304]{1,0:T(8,128)S(1)} %get-tuple-element.20.own, bf16[14,2304]{1,0:T(8,128)(2,1)S(1)} %collective-permute-done.8.refs_0_, bf16[14,2304]{1,0:T(8,128)(2,1)S(1)} %collective-permute-done.9.refs_1_, bf16[14,2304]{1,0:T(8,128)(2,1)S(1)} %collective-permute-done.10.refs_2_), custom_call_target="tpu_custom_call" | custom-call | tf_op jit(solution)/shard_map/pallas_call | solution.py:41
  (1 shorter events, 0.0 us)
Async XLA Ops:
  0.0 16.7 %collective-permute-start.4 = (bf16[3,256,2304]{2,1,0:T(8,128)(2,1)}, bf16[3,256,2304]{2,1,0:T(8,128)(2,1)S(1)}, u32[]{:S(2)}, u32[]{:S(2)}) collective-permute-start(bf16[3,256,2304]{2,1,0:T(8,128)(2,1)} %bitcast.2), channel_id=1, source_target_pairs={{0,1},{1,0},{2,3},{3,2},{4,5},{5,4},{6,7},{7,6},{8,9},{9,8},{10,11... | collective-permute-start | bytes 10616840 | tf_op jit(solution)/shard_map/ppermute | solution.py:24
  0.5 7.7 %collective-permute-start.2 = (bf16[2304,256]{1,0:T(8,128)(2,1)}, bf16[2304,256]{1,0:T(8,128)(2,1)S(1)}, u32[]{:S(2)}, u32[]{:S(2)}) collective-permute-start(bf16[2304,256]{1,0:T(8,128)(2,1)} %bitcast.3), channel_id=1, source_target_pairs={{0,1},{1,0},{2,3},{3,2},{4,5},{5,4},{6,7},{7,6},{8,9},{9,8},{10,11... | collective-permute-start | bytes 3538952 | tf_op jit(solution)/shard_map/ppermute | solution.py:24
  1.5 11.4 %collective-permute-start.1 = (bf16[2,14,2304]{2,1,0:T(8,128)(2,1)S(1)}, bf16[2,14,2304]{2,1,0:T(8,128)(2,1)S(1)}, u32[]{:S(2)}, u32[]{:S(2)}) collective-permute-start(bf16[2,14,2304]{2,1,0:T(8,128)(2,1)S(1)} %shard_map.73.refs_0_), channel_id=1, source_target_pairs={{0,8},{4,12},{8,0},{12,4},{1,9},{5,13},{9,1},{13,5},{2,10},{6,14},... | collective-permute-start | bytes 387080 | tf_op jit(solution)/shard_map/ppermute | solution.py:29
  5.6 7.9 %collective-permute-start = (bf16[2,14,2304]{2,1,0:T(8,128)(2,1)S(1)}, bf16[2,14,2304]{2,1,0:T(8,128)(2,1)S(1)}, u32[]{:S(2)}, u32[]{:S(2)}) collective-permute-start(bf16[2,14,2304]{2,1,0:T(8,128)(2,1)S(1)} %shard_map.73.refs_0_), channel_id=1, source_target_pairs={{0,4},{4,0},{8,12},{12,8},{1,5},{5,1},{9,13},{13,9},{2,6},{6,2},{1... | collective-permute-start | bytes 387080 | tf_op jit(solution)/shard_map/ppermute | solution.py:29
  12.8 5.1 %collective-permute-start.6 = (bf16[2,14,2304]{2,1,0:T(8,128)(2,1)S(1)}, bf16[2,14,2304]{2,1,0:T(8,128)(2,1)S(1)}, u32[]{:S(2)}, u32[]{:S(2)}) collective-permute-start(bf16[2,14,2304]{2,1,0:T(8,128)(2,1)S(1)} %collective-permute-done.1.refs_2_), channel_id=1, source_target_pairs={{0,4},{4,0},{8,12},{12,8},{1,5},{5,1},{9,13},{13,9},{2,6},{6,2},{1... | collective-permute-start | bytes 387080 | tf_op jit(solution)/shard_map/ppermute | solution.py:29
  13.5 1.2 %collective-permute-start.3 = (f32[2,256]{1,0:T(2,128)S(1)}, f32[2,256]{1,0:T(2,128)S(1)}, u32[]{:S(2)}, u32[]{:S(2)}) collective-permute-start(f32[2,256]{1,0:T(2,128)S(1)} %get-tuple-element.17.refs_3_.refs_2_), channel_id=1, source_target_pairs={{0,1},{1,0},{2,3},{3,2},{4,5},{5,4},{6,7},{7,6},{8,9},{9,8},{10,11... | collective-permute-start | bytes 6152 | tf_op jit(solution)/shard_map/ppermute | solution.py:24
  15.2 5.4 %collective-permute-start.5 = (bf16[3,14,512]{2,1,0:T(8,128)(2,1)S(1)}, bf16[3,14,512]{2,1,0:T(8,128)(2,1)S(1)}, u32[]{:S(2)}, u32[]{:S(2)}) collective-permute-start(bf16[3,14,512]{2,1,0:T(8,128)(2,1)S(1)} %shard_map.75.feats), channel_id=1, source_target_pairs={{0,2},{2,0},{1,3},{3,1},{4,6},{6,4},{5,7},{7,5},{8,10},{10,8},{9,1... | collective-permute-start | bytes 129032 | tf_op jit(solution)/shard_map/ppermute | solution.py:24
  18.5 2.0 %copy-start = (f32[1,2304]{1,0:T(1,128)S(1)}, f32[1,2304]{1,0:T(1,128)}, u32[]{:S(2)}) copy-start(f32[1,2304]{1,0:T(1,128)} %bias.5) | copy-start | bytes 27652
  18.5 5.0 %collective-permute-start.7 = (bf16[1,14,512]{2,1,0:T(8,128)(2,1)S(1)}, bf16[1,14,512]{2,1,0:T(8,128)(2,1)S(1)}, u32[]{:S(2)}, u32[]{:S(2)}) collective-permute-start(bf16[1,14,512]{2,1,0:T(8,128)(2,1)S(1)} %shard_map.77.feats), channel_id=1, source_target_pairs={{0,2},{2,0},{1,3},{3,1},{4,6},{6,4},{5,7},{7,5},{8,10},{10,8},{9,1... | collective-permute-start | bytes 43016 | tf_op jit(solution)/shard_map/ppermute | solution.py:24
  20.6 5.9 %collective-permute-start.9 = (bf16[14,2304]{1,0:T(8,128)(2,1)S(1)}, bf16[14,2304]{1,0:T(8,128)(2,1)S(1)}, u32[]{:S(2)}, u32[]{:S(2)}) collective-permute-start(bf16[14,2304]{1,0:T(8,128)(2,1)S(1)} %get-tuple-element.23), channel_id=1, source_target_pairs={{0,8},{4,12},{8,0},{12,4},{1,9},{5,13},{9,1},{13,5},{2,10},{6,14},... | collective-permute-start | bytes 193544 | tf_op jit(solution)/shard_map/ppermute | solution.py:29
  23.6 6.3 %collective-permute-start.8 = (bf16[14,2304]{1,0:T(8,128)(2,1)S(1)}, bf16[14,2304]{1,0:T(8,128)(2,1)S(1)}, u32[]{:S(2)}, u32[]{:S(2)}) collective-permute-start(bf16[14,2304]{1,0:T(8,128)(2,1)S(1)} %shard_map.80), channel_id=1, source_target_pairs={{0,12},{4,8},{8,4},{12,0},{1,13},{5,9},{9,5},{13,1},{2,14},{6,10},... | collective-permute-start | bytes 193544 | tf_op jit(solution)/shard_map/ppermute | solution.py:29
  26.5 4.4 %collective-permute-start.10 = (bf16[14,2304]{1,0:T(8,128)(2,1)S(1)}, bf16[14,2304]{1,0:T(8,128)(2,1)S(1)}, u32[]{:S(2)}, u32[]{:S(2)}) collective-permute-start(bf16[14,2304]{1,0:T(8,128)(2,1)S(1)} %get-tuple-element.24), channel_id=1, source_target_pairs={{0,4},{4,0},{8,12},{12,8},{1,5},{5,1},{9,13},{13,9},{2,6},{6,2},{1... | collective-permute-start | bytes 193544 | tf_op jit(solution)/shard_map/ppermute | solution.py:29
